TPU v7x, 32 devices: a whole 2x2x4 slice. The times are simulated.
32 devices in a mesh: dom: 8 (over y, x, core), sub: 4 (over z).
Axes of the slice: x: 2, y: 2, z: 4, core: 2. Of those that a mesh axis runs over, the one named last changes fastest.
Arguments:
- history: bfloat16 [1024, 64, 128], P(('dom', 'sub')), may hold values from -6 to 6
- send_list: int32 [32, 32, 1], P(('dom', 'sub')), may hold values from 0 to 31
- send_count: int32 [32, 32], P(('dom', 'sub')), may hold values from 0 to 1, as said below
- mixed_mass: bfloat16 [1024, 128, 128], P(('dom', 'sub')), may hold values from -0.5 to 0.5
- relay_list: int32 [32, 32, 1], P(('dom', 'sub')), may hold values from 0 to 31, as said below
- relay_target: int32 [32, 32, 1], P(('dom', 'sub')), may hold values from 0 to 63
- mass_diag: float32 [2048, 128, 128], P(('dom', 'sub')), as said below
- mass_next: float32 [2048, 128, 128], P(('dom', 'sub')), may hold values from -0.18 to 0.18
- coupling: int32 [2048], P(('dom', 'sub')), may hold values 0 or 1
- precond: float32 [2048, 128, 128], P(('dom', 'sub')), as said below
Outputs:
- solution: float32 [2048, 64, 128], P(('dom', 'sub'))
- residual: float32 [2048, 64, 128], P(('dom', 'sub'))
Inputs may be any that keep to these rules, and one draw needn't show every extreme that they name: `send_count`: live slots are the first ones. Every sender fills all 1 slots for some peer, and in every draw some receiver gets 1 live slots from every sender. For each owner e, the entries of relay_list[e] are a permutation of 0 .. 31. `mass_diag`: each block is symmetric; the assembled mass matrix is symmetric positive definite. `precond`: each block is symmetric positive definite.
All inputs are finite; a program needn't handle non-finite values. No bound on the sum of `coupling` on one device may be relied on, other than what follows from the above.
Results may differ from a plain program's by a relative error of at most 0.0003.
Values may be sent and summed in bfloat16 or wider, within the bound.
No kernel may reach another device: no remote copies, remote signals or barrier semaphores. Data moves between devices by JAX's collectives and lax.ppermute only.
A program may use at most 128 MiB of HBM per device.

v0:
```python
import functools

import jax
import jax.numpy as jnp
from jax import lax
from jax.experimental import pallas as pl
from jax.experimental.pallas import tpu as pltpu
from jax.sharding import PartitionSpec as P

AXES = ("dom", "sub")
EDGE = 3
EXTRA = 16
OCTAVE = 64.0
FULL = 32766.0
TINY = 1e-37
F32 = jnp.float32
BF16 = jnp.bfloat16
WHOLE = pl.BlockSpec(memory_space=pltpu.VMEM)
SCALARS = pl.BlockSpec(memory_space=pltpu.SMEM)


def params(mebibytes):
    return pltpu.CompilerParams(vmem_limit_bytes=mebibytes * 2**20)


def cost(flops, moved):
    return pl.CostEstimate(flops=int(flops), bytes_accessed=int(moved), transcendentals=0)


def dot(first, second):
    return jnp.dot(first, second, preferred_element_type=F32)


def parted(value):
    high = value.astype(BF16)
    return high, (value - high.astype(F32)).astype(BF16)


def tall(value):
    return jnp.concatenate(parted(value), axis=0)


def wide(value):
    return jnp.concatenate(parted(value), axis=1)


def by_wide(stacked, weights):
    rows, columns = stacked.shape[0] // 2, weights.shape[1] // 2
    out = dot(stacked, weights)
    return out[:rows, :columns] + (out[rows:, :columns] + out[:rows, columns:])


def by_pair(stacked, high, low):
    rows = stacked.shape[0] // 2
    out = dot(stacked, high)
    return out[:rows] + (out[rows:] + dot(stacked[:rows], low))


def pick_kernel(picks, counts, history, outgoing, *, slots):
    def step(entry, carry):
        live = (entry % slots) < counts[entry // slots]
        block = history[picks[entry]]
        outgoing[entry] = jnp.where(live, block, jnp.zeros_like(block))
        return carry

    total = outgoing.shape[0]
    lax.fori_loop(0, total, step, 0, unroll=8)


def prepare_kernel(coupling, diag, onward, precond, weights, pair_high, pair_low, cross, cross_t, trace, edges):
    step = pl.program_id(0)
    steps = pl.num_programs(0)
    blocks = diag.shape[0]
    rows = diag.shape[1]
    total = jnp.zeros((rows, rows), F32)
    for local in range(blocks):
        block = step * blocks + local
        own = diag[local]
        pre = precond[local]
        weights[block] = wide(pre)
        total = total + own * pre
    for local in range(blocks // 2):
        pair = step * (blocks // 2) + local
        linked = onward[2 * local] * coupling[2 * pair].astype(F32)
        whole = jnp.concatenate(
            [
                jnp.concatenate([diag[2 * local], linked], axis=1),
                jnp.concatenate([linked.T, diag[2 * local + 1]], axis=1),
            ],
            axis=0,
        )
        high, low = parted(whole)
        pair_high[pair] = high
        pair_low[pair] = low
        after = onward[2 * local + 1] * coupling[2 * pair + 1].astype(F32)
        cross[pair] = wide(after)
        cross_t[pair] = wide(after.T)
    part = total.reshape(rows // 8, 8, rows).sum(axis=0)

    @pl.when(step == 0)
    def _():
        trace[...] = part
        exact = functools.partial(jnp.dot, precision=lax.Precision.HIGHEST, preferred_element_type=F32)
        first = precond[0]
        edges[2] = first
        edges[3] = exact(exact(first, diag[0]), first)

    @pl.when(step > 0)
    def _():
        trace[...] += part

    @pl.when(step == steps - 1)
    def _():
        exact = functools.partial(jnp.dot, precision=lax.Precision.HIGHEST, preferred_element_type=F32)
        last = onward[blocks - 1] * coupling[steps * blocks - 1].astype(F32)
        mapped = exact(precond[blocks - 1], last)
        edges[0] = exact(last.T, mapped)
        edges[1] = exact(mapped.T, exact(diag[blocks - 1], mapped))


def mix_kernel(relay, arrived, mixing, trace, sending):
    total, values, rows = arrived.shape
    entries = trace.shape[0] * trace.shape[1]
    share = jnp.sum(jnp.sum(trace[...], axis=0, keepdims=True), axis=1, keepdims=True)
    share = jnp.maximum(jnp.broadcast_to(share, (1, rows)), TINY)
    share_code = jnp.floor(jnp.log2(share) * OCTAVE).astype(jnp.int32)
    lower = lax.broadcasted_iota(jnp.int32, (EXTRA, rows), 0) < EXTRA // 2

    def step(entry, carry):
        slot = relay[entry]
        tile = dot(arrived[slot], mixing[slot])
        peak = jnp.max(jnp.abs(tile), axis=0, keepdims=True)
        code = jnp.floor(jnp.log2(jnp.maximum(peak, TINY)) * OCTAVE) + 2.0
        scaled = tile * (FULL / jnp.exp2(code * (1.0 / OCTAVE)))
        scaled = jnp.clip(jnp.floor(scaled + 0.5), -32767.0, 32767.0)
        sending[entry, :values] = scaled.astype(jnp.int32).astype(jnp.int16)
        codes = jnp.where(lower, code.astype(jnp.int32), share_code)
        sending[entry, values:] = codes.astype(jnp.int16)
        return carry

    lax.fori_loop(0, total, step, 0, unroll=8)


def assemble_kernel(
    targets, received, weights, pair_high, pair_low, cross, cross_t, edges, rhs, theta_out, to_left, to_right, *, eigens
):
    total = received.shape[0]
    blocks, values, rows = rhs.shape
    rhs[...] = jnp.zeros_like(rhs)

    def step(entry, carry):
        extra = jnp.exp2(received[entry, values:].astype(jnp.int32).astype(F32) * (1.0 / OCTAVE))
        tile = received[entry, :values].astype(jnp.int32).astype(F32) * (extra[:1] * (1.0 / FULL))
        block = targets[entry]
        rhs[block] = rhs[block] + tile
        return carry + extra[EXTRA // 2 :]

    shares = lax.fori_loop(0, total, step, jnp.zeros((EXTRA // 2, rows), F32), unroll=8)
    theta = shares[:1] * (1.0 / eigens)
    theta_out[...] = jnp.broadcast_to(theta, theta_out.shape)
    pairs = blocks // 2

    def pre(value, block):
        return by_wide(tall(value), weights[block])

    both = functools.partial(jnp.concatenate, axis=1)
    first = [rhs[block] for block in range(EDGE)]
    z0 = [pre(first[block], block) for block in range(EDGE)]
    q1 = by_pair(tall(both(z0[:2])), pair_high[0], pair_low[0]) - both([theta, theta]) * both(first[:2])
    q1 = [q1[:, :rows], q1[:, rows:] + by_wide(tall(z0[2]), cross_t[0])]
    z1 = [pre(q1[block], block) for block in range(2)]
    q2 = by_pair(tall(both(z1)), pair_high[0], pair_low[0])[:, :rows] - theta * q1[0]
    to_left[0] = z0[0]
    to_left[1] = z1[0]
    to_left[2] = pre(q2, 0)
    last = [rhs[blocks - EDGE + block] for block in range(EDGE)]
    z0 = [pre(last[block], blocks - EDGE + block) for block in range(EDGE)]
    q1 = by_pair(tall(both(z0[1:])), pair_high[pairs - 1], pair_low[pairs - 1]) - both([theta, theta]) * both(last[1:])
    q1 = [q1[:, :rows] + by_wide(tall(z0[0]), cross[pairs - 2]), q1[:, rows:]]
    z1 = [pre(q1[block], blocks - 2 + block) for block in range(2)]
    q2 = by_pair(tall(both(z1)), pair_high[pairs - 1], pair_low[pairs - 1])[:, rows:] - theta * q1[1]
    for place, value in enumerate((z0[2], z1[1], pre(q2, blocks - 1))):
        to_right[place] = by_wide(tall(value), cross[pairs - 1])
    for half in range(2):
        part = slice(half * values, (half + 1) * values)
        to_right[3 + half] = edges[0, part]
        to_right[5 + half] = edges[1, part]
        to_left[3 + half] = edges[2, part]
        to_left[5 + half] = edges[3, part]


def basis_kernel(rhs, theta_in, weights, pair_high, pair_low, cross, cross_t, basis, mapped, sums, stacked):
    blocks, values, rows = rhs.shape
    pairs = blocks // 2
    theta = theta_in[:1]
    theta_pair = jnp.concatenate([theta, theta], axis=1)
    basis[0] = rhs[...]

    def sweep(level, carry):
        even = jnp.zeros((values, rows), F32)
        for block in range(blocks):
            value = basis[level, block]
            image = by_wide(tall(value), weights[block])
            mapped[level, block] = image
            high, low = parted(image)
            side = slice((block % 2) * rows, (block % 2 + 1) * rows)
            stacked[block // 2, :values, side] = high
            stacked[block // 2, values:, side] = low
            if EDGE <= block < blocks - EDGE:
                even = even + value * image
        sums[2 * level] = even
        odd = jnp.zeros((values, rows), F32)
        for pair in range(pairs):
            image = by_pair(stacked[pair], pair_high[pair], pair_low[pair])
            sides = [image[:, :rows], image[:, rows:]]
            if pair > 0:
                sides[0] = sides[0] + by_wide(stacked[pair - 1, :, rows:], cross[pair - 1])
            if pair < pairs - 1:
                sides[1] = sides[1] + by_wide(stacked[pair + 1, :, :rows], cross_t[pair])
            for side in range(2):
                block = 2 * pair + side
                value = sides[side] - theta * basis[level, block]
                basis[level + 1, block] = value
                if EDGE <= block < blocks - EDGE:
                    odd = odd + value * mapped[level, block]
        sums[2 * level + 1] = odd
        return carry

    lax.fori_loop(0, 3, sweep, 0)


def edge_kernel(
    from_left, from_right, basis, mapped, sums, theta_in, weights, pair_high, pair_low, cross, cross_t,
    basis_edge, mapped_edge, moments,
):
    _, blocks, values, rows = basis.shape
    pairs = blocks // 2
    theta = theta_in[:1]

    def pre(value, block):
        return by_wide(tall(value), weights[block])

    def pair_image(first, second, pair):
        out = by_pair(tall(jnp.concatenate([first, second], axis=1)), pair_high[pair], pair_low[pair])
        return out[:, :rows], out[:, rows:]

    def square(ref, place):
        return jnp.concatenate([ref[place], ref[place + 1]], axis=0)

    none = jnp.zeros((values, rows), F32)

    mirror = square(from_left, 3)
    second = square(from_left, 5) - theta * mirror
    mirror, second = wide(mirror), wide(second)
    start = tall(mapped[0, 0])
    dq1 = from_left[0]
    dz1 = pre(dq1, 0)
    z1 = mapped[1, 0] + dz1
    own, after = pair_image(dz1, none, 0)
    dq2 = (own - theta * dq1 + from_left[1] + by_wide(start, mirror), after)
    dz2 = (pre(dq2[0], 0), pre(dq2[1], 1))
    own, after = pair_image(dz2[0], dz2[1], 0)
    dq3 = (
        own - theta * dq2[0] + from_left[2] + by_wide(start, second) + by_wide(tall(z1), mirror),
        after - theta * dq2[1],
        by_wide(tall(dz2[1]), cross[0]),
    )
    changes = [((0, dq1),), ((0, dq2[0]), (1, dq2[1])), ((0, dq3[0]), (1, dq3[1]), (2, dq3[2]))]
    images = [((0, dz1),), ((0, dz2[0]), (1, dz2[1]))]

    last = blocks - 1
    pair = pairs - 1
    mirror = square(from_right, 3)
    second = square(from_right, 5) - theta * mirror
    mirror, second = wide(mirror), wide(second)
    start = tall(by_wide(tall(mapped[0, last]), cross[pair]))
    dq1 = by_wide(tall(from_right[0]), cross_t[pair])
    dz1 = pre(dq1, last)
    z1 = mapped[1, last] + dz1
    before, own = pair_image(none, dz1, pair)
    ahead = from_right[1] + by_wide(start, mirror)
    dq2 = (own - theta * dq1 + by_wide(tall(ahead), cross_t[pair]), before)
    dz2 = (pre(dq2[0], last), pre(dq2[1], last - 1))
    before, own = pair_image(dz2[1], dz2[0], pair)
    ahead = from_right[2] + by_wide(start, second) + by_wide(tall(by_wide(tall(z1), cross[pair])), mirror)
    dq3 = (
        own - theta * dq2[0] + by_wide(tall(ahead), cross_t[pair]),
        before - theta * dq2[1],
        by_wide(tall(dz2[1]), cross_t[pair - 1]),
    )
    changes[0] += ((5, dq1),)
    changes[1] += ((5, dq2[0]), (4, dq2[1]))
    changes[2] += ((5, dq3[0]), (4, dq3[1]), (3, dq3[2]))
    images[0] += ((5, dz1),)
    images[1] += ((5, dz2[0]), (4, dz2[1]))

    places = [0, 1, 2, blocks - 3, blocks - 2, blocks - 1]
    before = [rhs_block for rhs_block in (basis[0, block] for block in places)]
    lane = lax.broadcasted_iota(jnp.int32, (values, rows), 1)
    table = none
    for level in range(3):
        image = [mapped[level, block] for block in places]
        if level > 0:
            for place, change in images[level - 1]:
                image[place] = image[place] + change
            for place in range(2 * EDGE):
                mapped_edge[level - 1, place] = image[place]
        now = [basis[level + 1, block] for block in places]
        for place, change in changes[level]:
            now[place] = now[place] + change
        even = sums[2 * level]
        odd = sums[2 * level + 1]
        for place in range(2 * EDGE):
            basis_edge[level, place] = now[place]
            even = even + before[place] * image[place]
            odd = odd + now[place] * image[place]
        table = jnp.where(lane == 2 * level, jnp.sum(even, axis=1, keepdims=True), table)
        table = jnp.where(lane == 2 * level + 1, jnp.sum(odd, axis=1, keepdims=True), table)
        before = now
    flipped = jnp.concatenate([table, jnp.zeros((rows - values, rows), F32)], axis=0).T[:8]
    for peer in range(moments.shape[0]):
        moments[peer] = flipped


def combine_kernel(moments, theta_in, basis, mapped, basis_edge, mapped_edge, solution, residual, factors):
    step = pl.program_id(0)
    _, blocks, values, rows = basis.shape
    chunk = solution.shape[0]

    @pl.when(step == 0)
    def _():
        total = jnp.sum(moments[...], axis=0)
        theta = theta_in[:1]
        m0, m1, m2, m3, m4, m5 = (total[place : place + 1] for place in range(6))
        m0 = m0 + TINY
        l10 = m1 / m0
        l20 = m2 / m0
        d1 = m2 - l10 * m1 + TINY
        g21 = m3 - l20 * m1
        l21 = g21 / d1
        d2 = m4 - l20 * m2 - l21 * g21 + TINY
        b1 = l10 * m3 - m4
        b2 = l20 * m3 - l21 * b1 - m5
        c2 = b2 / d2
        c1 = b1 / d1 - l21 * c2
        c0 = -m3 / m0 - l10 * c1 - l20 * c2
        scale = 1.0 / (c0 - theta * (c1 - theta * (c2 - theta)))
        c0, c1, c2, c3 = c0 * scale, c1 * scale, c2 * scale, scale
        y2 = -c3
        y1 = -c2 - theta * y2
        y0 = -c1 - theta * y1
        table = jnp.concatenate([c0, c1, c2, c3, y0, y1, y2, jnp.zeros((rows - 7, rows), F32)], axis=0).T
        for place in range(7):
            factors[place] = jnp.broadcast_to(table[:values, place : place + 1], (values, rows))

    factor = [factors[place] for place in range(7)]

    def store(place, q, z):
        residual[place] = (q[0] * factor[0] + q[1] * factor[1]) + (q[2] * factor[2] + q[3] * factor[3])
        solution[place] = z[0] * factor[4] + z[1] * factor[5] + z[2] * factor[6]

    for place in range(chunk):
        block = step * chunk + place
        store(place, [basis[level, block] for level in range(4)], [mapped[level, block] for level in range(3)])

    def edge(place, block, entry):
        q = [basis[0, block]] + [basis_edge[level, entry] for level in range(3)]
        z = [mapped[0, block]] + [mapped_edge[level, entry] for level in range(2)]
        store(place, q, z)

    @pl.when(step == 0)
    def _():
        for entry in range(EDGE):
            edge(entry, entry, entry)

    @pl.when(step == pl.num_programs(0) - 1)
    def _():
        for entry in range(EDGE):
            edge(chunk - EDGE + entry, blocks - EDGE + entry, EDGE + entry)


def shifted(value, steps):
    count = lax.axis_size(AXES)
    first, last = (max(0, -steps), min(count, count - steps))
    return lax.ppermute(value, AXES, [(source, source + steps) for source in range(first, last)])


def body(
    history,
    send_list,
    send_count,
    mixed_mass,
    relay_list,
    relay_target,
    mass_diag,
    mass_next,
    coupling,
    precond,
):
    devices = lax.axis_size(AXES)
    slots = send_list.shape[2]
    total = devices * slots
    values, rows = history.shape[1:]
    blocks = mass_diag.shape[0]
    pairs = blocks // 2
    field = (blocks, values, rows)
    unit = 2 * values * rows * rows

    outgoing = pl.pallas_call(
        functools.partial(pick_kernel, slots=slots),
        out_shape=jax.ShapeDtypeStruct((total, values, rows), BF16),
        in_specs=[SCALARS, SCALARS, WHOLE],
        out_specs=WHOLE,
        compiler_params=params(16),
        name="pick",
    )(send_list.reshape(-1), send_count.reshape(-1), history)
    arrived = lax.all_to_all(outgoing, AXES, split_axis=0, concat_axis=0, tiled=True)

    chunk = 8
    matrix = pl.BlockSpec((chunk, rows, rows), lambda step: (step, 0, 0))
    weights, pair_high, pair_low, cross, cross_t, trace, edges = pl.pallas_call(
        prepare_kernel,
        grid=(blocks // chunk,),
        out_shape=(
            pltpu.VMEM((blocks, rows, 2 * rows), BF16),
            pltpu.VMEM((pairs, 2 * rows, 2 * rows), BF16),
            pltpu.VMEM((pairs, 2 * rows, 2 * rows), BF16),
            pltpu.VMEM((pairs, rows, 2 * rows), BF16),
            pltpu.VMEM((pairs, rows, 2 * rows), BF16),
            pltpu.VMEM((8, rows), F32),
            pltpu.VMEM((4, rows, rows), F32),
        ),
        in_specs=[SCALARS, matrix, matrix, matrix],
        out_specs=(WHOLE,) * 7,
        compiler_params=params(16),
        cost_estimate=cost(0, 28 * 2**20),
        name="prepare",
    )(coupling, mass_diag, mass_next, precond)
    operator = (weights, pair_high, pair_low, cross, cross_t)

    sending = pl.pallas_call(
        mix_kernel,
        out_shape=jax.ShapeDtypeStruct((total, values + EXTRA, rows), jnp.int16),
        in_specs=[SCALARS, WHOLE, WHOLE, WHOLE],
        out_specs=WHOLE,
        compiler_params=params(16),
        name="mix",
    )(relay_list.reshape(-1), arrived, mixed_mass, trace)
    received = lax.all_to_all(sending, AXES, split_axis=0, concat_axis=0, tiled=True)

    ends = jax.ShapeDtypeStruct((EDGE + 4, values, rows), F32)
    rhs, theta, to_left, to_right = pl.pallas_call(
        functools.partial(assemble_kernel, eigens=devices * blocks * rows),
        out_shape=(pltpu.VMEM(field, F32), pltpu.VMEM((8, rows), F32), ends, ends),
        in_specs=[SCALARS] + [WHOLE] * 7,
        out_specs=(WHOLE,) * 4,
        compiler_params=params(16),
        name="assemble",
    )(relay_target.reshape(-1), received, *operator, edges)
    from_right = shifted(to_left, -1)
    from_left = shifted(to_right, 1)

    basis, mapped, sums = pl.pallas_call(
        basis_kernel,
        out_shape=(pltpu.VMEM((4,) + field, F32), pltpu.VMEM((3,) + field, F32), pltpu.VMEM((6, values, rows), F32)),
        in_specs=[WHOLE] * 7,
        out_specs=(WHOLE,) * 3,
        scratch_shapes=[pltpu.VMEM((pairs, 2 * values, 2 * rows), BF16)],
        compiler_params=params(16),
        cost_estimate=cost(36 * blocks * unit, 32 * 2**20),
        name="basis",
    )(rhs, theta, *operator)

    basis_edge, mapped_edge, moments = pl.pallas_call(
        edge_kernel,
        out_shape=(
            pltpu.VMEM((3, 2 * EDGE, values, rows), F32),
            pltpu.VMEM((2, 2 * EDGE, values, rows), F32),
            jax.ShapeDtypeStruct((devices, 8, rows), F32),
        ),
        in_specs=[WHOLE] * 11,
        out_specs=(WHOLE,) * 3,
        compiler_params=params(16),
        name="edge",
    )(from_left, from_right, basis, mapped, sums, theta, *operator)
    gathered = lax.all_to_all(moments, AXES, split_axis=0, concat_axis=0, tiled=True)

    result = pl.BlockSpec((chunk, values, rows), lambda step: (step, 0, 0))
    return pl.pallas_call(
        combine_kernel,
        grid=(blocks // chunk,),
        out_shape=(jax.ShapeDtypeStruct(field, F32),) * 2,
        in_specs=[WHOLE] * 6,
        out_specs=(result, result),
        scratch_shapes=[pltpu.VMEM((7, values, rows), F32)],
        compiler_params=params(16),
        name="combine",
    )(gathered, theta, basis, mapped, basis_edge, mapped_edge)


def solution(mesh):
    placed = (
        P(AXES, None, None),
        P(AXES, None, None),
        P(AXES, None),
        P(AXES, None, None),
        P(AXES, None, None),
        P(AXES, None, None),
        P(AXES, None, None),
        P(AXES, None, None),
        P(AXES),
        P(AXES, None, None),
    )
    return jax.shard_map(
        body,
        mesh=mesh,
        in_specs=placed,
        out_specs=(P(AXES, None, None), P(AXES, None, None)),
        check_vma=False,
    )
```

profile of v0, /device:TPU:0, one launch (start us, length us, event | category | flops | bytes accessed | tf_op | source)
XLA Modules:
  0.0 102.2 jit_solution(15585425046394027520)
XLA Ops:
  0.6 0.0 copy-start.12
  0.6 1.0 %copy-done.12 = bf16[32,64,128]{2,1,0:T(8,128)(2,1)S(1)} copy-done((bf16[32,64,128]{2,1,0:T(8,128)(2,1)S(1)}, bf16[32,64,128]{2,1,0:T(8,128)(2,1)}, u32[]{:S(2)}) %copy-start.12) | copy-done | bytes 524312
  1.7 0.0 copy-start.14
  1.7 0.7 copy-done.14
  2.3 0.0 copy-start.15
  2.3 0.7 copy-done.15
  3.0 1.5 %pick.1 = bf16[32,64,128]{2,1,0:T(8,128)(2,1)} custom-call(s32[32]{0:T(128)S(1)} %bitcast.5, s32[32]{0:T(128)S(1)} %bitcast.6, bf16[32,64,128]{2,1,0:T(8,128)(2,1)S(1)} %copy-done.12), custom_call_target="tpu_custom_call" | custom-call | tf_op jit(solution)/shard_map/pick/pallas_call | solution.py:409
  4.5 7.3 %all-to-all-start = ((bf16[32,64,128]{2,1,0:T(8,128)(2,1)}), bf16[32,64,128]{2,1,0:T(8,128)(2,1)S(1)}, u32[]{:S(2)}, u32[]{:S(2)}) async-start(bf16[32,64,128]{2,1,0:T(8,128)(2,1)} %pick.1), calls=%async_computation | async-start | bytes 1048576 | tf_op jit(solution)/shard_map/all_to_all | solution.py:417
  11.8 0.0 copy-start.8
  11.8 2.2 %copy-done.8 = f32[64,128,128]{2,1,0:T(8,128)S(1)} copy-done((f32[64,128,128]{2,1,0:T(8,128)S(1)}, f32[64,128,128]{2,1,0:T(8,128)}, u32[]{:S(2)}) %copy-start.8) | copy-done | bytes 4194328
  14.0 0.0 copy-start.9
  14.0 2.2 %copy-done.9 = f32[64,128,128]{2,1,0:T(8,128)S(1)} copy-done((f32[64,128,128]{2,1,0:T(8,128)S(1)}, f32[64,128,128]{2,1,0:T(8,128)}, u32[]{:S(2)}) %copy-start.9) | copy-done | bytes 4194328
  16.2 0.0 copy-start.10
  16.2 2.2 %copy-done.10 = f32[64,128,128]{2,1,0:T(8,128)S(1)} copy-done((f32[64,128,128]{2,1,0:T(8,128)S(1)}, f32[64,128,128]{2,1,0:T(8,128)}, u32[]{:S(2)}) %copy-start.10) | copy-done | bytes 4194328
  18.4 0.0 copy-start.16
  18.4 0.7 copy-done.16
  19.0 0.0 copy-start.17
  19.0 0.0 copy-start.13
  19.0 4.4 %prepare.1 = (bf16[64,128,256]{2,1,0:T(8,128)(2,1)S(1)}, bf16[32,256,256]{2,1,0:T(8,128)(2,1)S(1)}, bf16[32,256,256]{2,1,0:T(8,128)(2,1)S(1)}, bf16[32,128,256]{...) custom-call(s32[64]{0:T(128)S(1)} %copy-done.16, ...), custom_call_target="tpu_custom_call" | custom-call | bytes 29360128 | tf_op jit(solution)/shard_map/prepare/pallas_call | solution.py:421
  23.4 0.0 copy-start
  23.5 1.9 %copy-done = bf16[64,128,256]{2,1,0:T(8,128)(2,1)} copy-done((bf16[64,128,256]{2,1,0:T(8,128)(2,1)}, bf16[64,128,256]{2,1,0:T(8,128)(2,1)S(1)}, u32[]{:S(2)}) %copy-start) | copy-done | bytes 4194328
  25.4 0.0 copy-start.2
  25.4 2.0 %copy-done.2 = bf16[32,256,256]{2,1,0:T(8,128)(2,1)} copy-done((bf16[32,256,256]{2,1,0:T(8,128)(2,1)}, bf16[32,256,256]{2,1,0:T(8,128)(2,1)S(1)}, u32[]{:S(2)}) %copy-start.2) | copy-done | bytes 4194328
  27.4 0.0 copy-start.4
  27.4 2.0 %copy-done.4 = bf16[32,256,256]{2,1,0:T(8,128)(2,1)} copy-done((bf16[32,256,256]{2,1,0:T(8,128)(2,1)}, bf16[32,256,256]{2,1,0:T(8,128)(2,1)S(1)}, u32[]{:S(2)}) %copy-start.4) | copy-done | bytes 4194328
  29.4 0.0 copy-start.6
  29.4 1.3 %copy-done.6 = bf16[32,128,256]{2,1,0:T(8,128)(2,1)} copy-done((bf16[32,128,256]{2,1,0:T(8,128)(2,1)}, bf16[32,128,256]{2,1,0:T(8,128)(2,1)S(1)}, u32[]{:S(2)}) %copy-start.6) | copy-done | bytes 2097176
  30.7 0.0 all-to-all-done.arrived
  30.7 0.0 copy-start.7
  30.7 0.0 copy-done.17
  30.7 0.0 copy-start.11
  30.7 1.4 %copy-done.11 = bf16[32,128,128]{2,1,0:T(8,128)(2,1)S(1)} copy-done((bf16[32,128,128]{2,1,0:T(8,128)(2,1)S(1)}, bf16[32,128,128]{2,1,0:T(8,128)(2,1)}, u32[]{:S(2)}) %copy-start.11) | copy-done | bytes 1048600
  32.1 1.8 %mix.1 = s16[32,80,128]{2,1,0:T(8,128)(2,1)S(1)} custom-call(s32[32]{0:T(128)S(1)} %bitcast.7, bf16[32,64,128]{2,1,0:T(8,128)(2,1)S(1)} %all-to-all-done.arrived, bf16[32,128,128]{2,1,0:T(8,128)(2,1)S(1)} %copy-done.11, f32[8,128]{1,0:T(8,128)S(1)} %get-tuple-element.19.trace), custom_call_target="tpu_custom_call" | custom-call | tf_op jit(solution)/shard_map/mix/pallas_call | solution.py:441
  33.9 22.6 %all_to_all.15.received = s16[32,80,128]{2,1,0:T(8,128)(2,1)S(1)} all-to-all(s16[32,80,128]{2,1,0:T(8,128)(2,1)S(1)} %mix.1), channel_id=1, replica_groups=mesh['dom'=8,'sub'=4] {'dom','sub'}, dimensions={0} | all-to-all | bytes 1310720 | tf_op jit(solution)/shard_map/all_to_all | solution.py:449
  56.4 0.0 copy-done.13
  56.4 0.0 copy-done.7
  56.4 0.0 copy-start.1
  56.4 2.2 %copy-done.1 = bf16[64,128,256]{2,1,0:T(8,128)(2,1)S(1)} copy-done((bf16[64,128,256]{2,1,0:T(8,128)(2,1)S(1)}, bf16[64,128,256]{2,1,0:T(8,128)(2,1)}, u32[]{:S(2)}) %copy-start.1) | copy-done | bytes 4194328
  58.6 0.0 copy-start.3
  58.6 2.2 %copy-done.3 = bf16[32,256,256]{2,1,0:T(8,128)(2,1)S(1)} copy-done((bf16[32,256,256]{2,1,0:T(8,128)(2,1)S(1)}, bf16[32,256,256]{2,1,0:T(8,128)(2,1)}, u32[]{:S(2)}) %copy-start.3) | copy-done | bytes 4194328
  60.8 0.0 copy-start.5
  60.8 2.2 %copy-done.5 = bf16[32,256,256]{2,1,0:T(8,128)(2,1)S(1)} copy-done((bf16[32,256,256]{2,1,0:T(8,128)(2,1)S(1)}, bf16[32,256,256]{2,1,0:T(8,128)(2,1)}, u32[]{:S(2)}) %copy-start.5) | copy-done | bytes 4194328
  63.0 2.5 %assemble.1 = (f32[64,64,128]{2,1,0:T(8,128)S(1)}, f32[8,128]{1,0:T(8,128)S(1)}, f32[7,64,128]{2,1,0:T(8,128)S(1)}, f32[7,64,128]{2,1,0:T(8,128)S(1)}) custom-call(s32[32]{0:T(128)S(1)} %bitcast.4, s16[32,80,128]{2,1,0:T(8,128)(2,1)S(1)} %all_to_all.15.received, bf16[64,128,256]{2,1,0:T(8,128)(2,1)S(1)} %copy-done.1, bf16[32,256,256]{2,1,0:T(8,128)(2,1)S(1)} %copy-done.3, ...), custom_call_target="tpu_custom_call" | custom-call | tf_op jit(solution)/shard_map/assemble/pallas_call | solution.py:452
  65.5 4.7 %collective-permute-start = (f32[7,64,128]{2,1,0:T(8,128)S(1)}, f32[7,64,128]{2,1,0:T(8,128)S(1)}, u32[]{:S(2)}, u32[]{:S(2)}) collective-permute-start(f32[7,64,128]{2,1,0:T(8,128)S(1)} %get-tuple-element.26), channel_id=1, source_target_pairs={{0,1},{1,2},{2,3},{3,4},{4,5},{5,6},{6,7},{7,8},{8,9},{9,10},{10,1... | collective-permute-start | bytes 688136 | tf_op jit(solution)/shard_map/ppermute | solution.py:385
  70.3 1.3 %collective-permute-start.1 = (f32[7,64,128]{2,1,0:T(8,128)S(1)}, f32[7,64,128]{2,1,0:T(8,128)S(1)}, u32[]{:S(2)}, u32[]{:S(2)}) collective-permute-start(f32[7,64,128]{2,1,0:T(8,128)S(1)} %get-tuple-element.27), channel_id=1, source_target_pairs={{1,0},{2,1},{3,2},{4,3},{5,4},{6,5},{7,6},{8,7},{9,8},{10,9},{11,1... | collective-permute-start | bytes 688136 | tf_op jit(solution)/shard_map/ppermute | solution.py:385
  71.6 11.2 %basis.1 = (f32[4,64,64,128]{3,2,1,0:T(8,128)S(1)}, f32[3,64,64,128]{3,2,1,0:T(8,128)S(1)}, f32[6,64,128]{2,1,0:T(8,128)S(1)}) custom-call(f32[64,64,128]{2,1,0:T(8,128)S(1)} %get-tuple-element.28.rhs, f32[8,128]{1,0:T(8,128)S(1)} %get-tuple-element.29.theta_in, bf16[64,128,256]{2,1,0:T(8,128)(2,1)S(1)} %copy-done.1, bf16[32,256,256]{2,1,0:T(8,128)(2,1)S(1)} %copy-done.3, ...), custom_call_target="tpu_custom_call" | custom-call | flops 4831838208 | bytes 33554432 | tf_op jit(solution)/shard_map/basis/pallas_call | solution.py:463
  82.7 0.0 collective-permute-done.from_left
  82.8 0.2 collective-permute-done.1.from_right
  83.0 1.8 %edge.1 = (f32[3,6,64,128]{3,2,1,0:T(8,128)S(1)}, f32[2,6,64,128]{3,2,1,0:T(8,128)S(1)}, f32[32,8,128]{2,1,0:T(8,128)S(1)}) custom-call(f32[7,64,128]{2,1,0:T(8,128)S(1)} %collective-permute-done.from_left, f32[7,64,128]{2,1,0:T(8,128)S(1)} %collective-permute-done.1.from_right, f32[4,64,64,128]{3,2,1,0:T(8,128)S(1)} %get-tuple-element.30.basis, ...), custom_call_target="tpu_custom_call" | custom-call | tf_op jit(solution)/shard_map/edge/pallas_call | solution.py:474
  84.7 13.0 %all_to_all.16.moments = f32[32,8,128]{2,1,0:T(8,128)S(1)} all-to-all(f32[32,8,128]{2,1,0:T(8,128)S(1)} %get-tuple-element.33), channel_id=1, replica_groups=mesh['dom'=8,'sub'=4] {'dom','sub'}, dimensions={0} | all-to-all | bytes 262144 | tf_op jit(solution)/shard_map/all_to_all | solution.py:486
  97.8 4.4 %combine.1 = (f32[64,64,128]{2,1,0:T(8,128)}, f32[64,64,128]{2,1,0:T(8,128)}) custom-call(f32[32,8,128]{2,1,0:T(8,128)S(1)} %all_to_all.16.moments, f32[8,128]{1,0:T(8,128)S(1)} %get-tuple-element.29.theta_in, f32[4,64,64,128]{3,2,1,0:T(8,128)S(1)} %get-tuple-element.30.basis, f32[3,64,64,128]{3,2,1,0:T(8,128)S(1)} %get-tuple-element.31.mapped, ...), custom_call_target="tpu_custom_call" | custom-call | tf_op jit(solution)/shard_map/combine/pallas_call | solution.py:489
Async XLA Ops:
  0.6 1.0 %copy-start.12 = (bf16[32,64,128]{2,1,0:T(8,128)(2,1)S(1)}, bf16[32,64,128]{2,1,0:T(8,128)(2,1)}, u32[]{:S(2)}) copy-start(bf16[32,64,128]{2,1,0:T(8,128)(2,1)} %history.1) | copy-start | bytes 1572868
  1.7 0.7 copy-start.14
  2.3 0.7 copy-start.15
  4.5 26.2 %all-to-all-start = ((bf16[32,64,128]{2,1,0:T(8,128)(2,1)}), bf16[32,64,128]{2,1,0:T(8,128)(2,1)S(1)}, u32[]{:S(2)}, u32[]{:S(2)}) async-start(bf16[32,64,128]{2,1,0:T(8,128)(2,1)} %pick.1), calls=%async_computation | async-start | bytes 1048576 | tf_op jit(solution)/shard_map/all_to_all | solution.py:417
  11.8 2.2 %copy-start.8 = (f32[64,128,128]{2,1,0:T(8,128)S(1)}, f32[64,128,128]{2,1,0:T(8,128)}, u32[]{:S(2)}) copy-start(f32[64,128,128]{2,1,0:T(8,128)} %diag.1) | copy-start | bytes 12582916
  14.0 2.2 %copy-start.9 = (f32[64,128,128]{2,1,0:T(8,128)S(1)}, f32[64,128,128]{2,1,0:T(8,128)}, u32[]{:S(2)}) copy-start(f32[64,128,128]{2,1,0:T(8,128)} %onward.1) | copy-start | bytes 12582916
  16.2 2.2 %copy-start.10 = (f32[64,128,128]{2,1,0:T(8,128)S(1)}, f32[64,128,128]{2,1,0:T(8,128)}, u32[]{:S(2)}) copy-start(f32[64,128,128]{2,1,0:T(8,128)} %precond.1) | copy-start | bytes 12582916
  18.4 0.7 copy-start.16
  19.0 11.7 %copy-start.17 = (s32[1,32,1]{1,2,0:T(1,128)S(1)}, s32[1,32,1]{1,2,0:T(1,128)}, u32[]{:S(2)}) copy-start(s32[1,32,1]{1,2,0:T(1,128)} %param.14) | copy-start | bytes 388
  19.0 37.4 %copy-start.13 = (s32[1,32,1]{1,2,0:T(1,128)S(1)}, s32[1,32,1]{1,2,0:T(1,128)}, u32[]{:S(2)}) copy-start(s32[1,32,1]{1,2,0:T(1,128)} %param.15) | copy-start | bytes 388
  23.4 1.9 %copy-start = (bf16[64,128,256]{2,1,0:T(8,128)(2,1)}, bf16[64,128,256]{2,1,0:T(8,128)(2,1)S(1)}, u32[]{:S(2)}) copy-start(bf16[64,128,256]{2,1,0:T(8,128)(2,1)S(1)} %get-tuple-element.20.weights) | copy-start | bytes 12582916
  25.4 2.0 %copy-start.2 = (bf16[32,256,256]{2,1,0:T(8,128)(2,1)}, bf16[32,256,256]{2,1,0:T(8,128)(2,1)S(1)}, u32[]{:S(2)}) copy-start(bf16[32,256,256]{2,1,0:T(8,128)(2,1)S(1)} %get-tuple-element.21.pair_high) | copy-start | bytes 12582916
  27.4 2.0 %copy-start.4 = (bf16[32,256,256]{2,1,0:T(8,128)(2,1)}, bf16[32,256,256]{2,1,0:T(8,128)(2,1)S(1)}, u32[]{:S(2)}) copy-start(bf16[32,256,256]{2,1,0:T(8,128)(2,1)S(1)} %get-tuple-element.22.pair_low) | copy-start | bytes 12582916
  29.4 1.3 %copy-start.6 = (bf16[32,128,256]{2,1,0:T(8,128)(2,1)}, bf16[32,128,256]{2,1,0:T(8,128)(2,1)S(1)}, u32[]{:S(2)}) copy-start(bf16[32,128,256]{2,1,0:T(8,128)(2,1)S(1)} %get-tuple-element.24.cross_t) | copy-start | bytes 6291460
  30.7 25.7 %copy-start.7 = (bf16[32,128,256]{2,1,0:T(8,128)(2,1)S(1)}, bf16[32,128,256]{2,1,0:T(8,128)(2,1)}, u32[]{:S(2)}) copy-start(bf16[32,128,256]{2,1,0:T(8,128)(2,1)} %copy-done.6) | copy-start | bytes 6291460
  30.7 1.4 %copy-start.11 = (bf16[32,128,128]{2,1,0:T(8,128)(2,1)S(1)}, bf16[32,128,128]{2,1,0:T(8,128)(2,1)}, u32[]{:S(2)}) copy-start(bf16[32,128,128]{2,1,0:T(8,128)(2,1)} %mixing.1) | copy-start | bytes 3145732
  56.4 2.2 %copy-start.1 = (bf16[64,128,256]{2,1,0:T(8,128)(2,1)S(1)}, bf16[64,128,256]{2,1,0:T(8,128)(2,1)}, u32[]{:S(2)}) copy-start(bf16[64,128,256]{2,1,0:T(8,128)(2,1)} %copy-done) | copy-start | bytes 12582916
  58.6 2.2 %copy-start.3 = (bf16[32,256,256]{2,1,0:T(8,128)(2,1)S(1)}, bf16[32,256,256]{2,1,0:T(8,128)(2,1)}, u32[]{:S(2)}) copy-start(bf16[32,256,256]{2,1,0:T(8,128)(2,1)} %copy-done.2) | copy-start | bytes 12582916
  60.8 2.2 %copy-start.5 = (bf16[32,256,256]{2,1,0:T(8,128)(2,1)S(1)}, bf16[32,256,256]{2,1,0:T(8,128)(2,1)}, u32[]{:S(2)}) copy-start(bf16[32,256,256]{2,1,0:T(8,128)(2,1)} %copy-done.4) | copy-start | bytes 12582916
  65.5 17.2 %collective-permute-start = (f32[7,64,128]{2,1,0:T(8,128)S(1)}, f32[7,64,128]{2,1,0:T(8,128)S(1)}, u32[]{:S(2)}, u32[]{:S(2)}) collective-permute-start(f32[7,64,128]{2,1,0:T(8,128)S(1)} %get-tuple-element.26), channel_id=1, source_target_pairs={{0,1},{1,2},{2,3},{3,4},{4,5},{5,6},{6,7},{7,8},{8,9},{9,10},{10,1... | collective-permute-start | bytes 688136 | tf_op jit(solution)/shard_map/ppermute | solution.py:385
  70.3 12.7 %collective-permute-start.1 = (f32[7,64,128]{2,1,0:T(8,128)S(1)}, f32[7,64,128]{2,1,0:T(8,128)S(1)}, u32[]{:S(2)}, u32[]{:S(2)}) collective-permute-start(f32[7,64,128]{2,1,0:T(8,128)S(1)} %get-tuple-element.27), channel_id=1, source_target_pairs={{1,0},{2,1},{3,2},{4,3},{5,4},{6,5},{7,6},{8,7},{9,8},{10,9},{11,1... | collective-permute-start | bytes 688136 | tf_op jit(solution)/shard_map/ppermute | solution.py:385
where the time goes:
time: 103 us; the launch traced here: 102 us
  blocking collectives  35.6 us (35%)
  Pallas kernels  27.6 us (27%)
  local copies, waits for them, and re-layouts  24.7 us (24%)
  starting transfers between devices  13.3 us (13%)
    unnamed x36, local copies, waits for them, and re-layouts  24.7 us
    all_to_all x1, blocking collectives, body(): lax.all_to_all(sending, AXES, split_axis=0, concat_axis=0, tiled=True)  22.6 us
    all_to_all x1, blocking collectives, body(): lax.all_to_all(moments, AXES, split_axis=0, concat_axis=0, tiled=True)  13 us
    pallas_call x1, Pallas kernels, body(): pl.pallas_call(basis_kernel, out_shape=(pltpu.VMEM((4,) + field, F32), pl...  11.2 us
    all_to_all x1, starting transfers between devices, body(): lax.all_to_all(outgoing, AXES, split_axis=0, concat_axis=0, tiled=True)  7.3 us
    ppermute x2, starting transfers between devices, shifted(): lax.ppermute(value, AXES, [(source, source + steps) for source in range(f...  6.02 us
    pallas_call x1, Pallas kernels, body(): pl.pallas_call(combine_kernel, grid=(blocks // chunk,), out_shape=(jax.Sh...  4.44 us
    pallas_call x1, Pallas kernels, body(): pl.pallas_call(prepare_kernel, grid=(blocks // chunk,), out_shape=(pltpu....  4.42 us
  transfers between devices with their start and end apart: 3, of which 1 were waited for; matrix products, arithmetic and copies ran while one was open for 0% of the time, Pallas kernels for 15%

commit v1 on v0

--- a/solution.py
+++ b/solution.py
@@ -9,13 +9,14 @@
 
 AXES = ("dom", "sub")
 EDGE = 3
-EXTRA = 16
+EXTRA = 8
 OCTAVE = 64.0
 FULL = 32766.0
 TINY = 1e-37
 F32 = jnp.float32
 BF16 = jnp.bfloat16
 WHOLE = pl.BlockSpec(memory_space=pltpu.VMEM)
+AWAY = pl.BlockSpec(memory_space=pl.ANY)
 SCALARS = pl.BlockSpec(memory_space=pltpu.SMEM)
 
 
@@ -25,6 +26,13 @@
 
 def cost(flops, moved):
     return pl.CostEstimate(flops=int(flops), bytes_accessed=int(moved), transcendentals=0)
+
+
+def layout(rows):
+    def place(first, count):
+        return slice(first * rows, (first + count) * rows)
+
+    return (place(0, 1), place(1, 1)), place(2, 2), place(0, 2), place(2, 1), place(3, 1)
 
 
 def dot(first, second):
@@ -67,20 +75,19 @@
     lax.fori_loop(0, total, step, 0, unroll=8)
 
 
-def prepare_kernel(coupling, diag, onward, precond, weights, pair_high, pair_low, cross, cross_t, trace, edges):
+def prepare_kernel(coupling, diag, onward, precond, near, far, near_ends, far_ends, beside, trace, edges):
     step = pl.program_id(0)
     steps = pl.num_programs(0)
     blocks = diag.shape[0]
     rows = diag.shape[1]
+    pre, high, low, cross, cross_t = layout(rows)
     total = jnp.zeros((rows, rows), F32)
-    for local in range(blocks):
-        block = step * blocks + local
-        own = diag[local]
-        pre = precond[local]
-        weights[block] = wide(pre)
-        total = total + own * pre
     for local in range(blocks // 2):
         pair = step * (blocks // 2) + local
+        for side in range(2):
+            own = precond[2 * local + side]
+            near[local, pre[side]] = wide(own)
+            total = total + own * diag[2 * local + side]
         linked = onward[2 * local] * coupling[2 * pair].astype(F32)
         whole = jnp.concatenate(
             [
@@ -89,18 +96,19 @@
             ],
             axis=0,
         )
-        high, low = parted(whole)
-        pair_high[pair] = high
-        pair_low[pair] = low
-        after = onward[2 * local + 1] * coupling[2 * pair + 1].astype(F32)
-        cross[pair] = wide(after)
-        cross_t[pair] = wide(after.T)
+        near[local, high], far[local, low] = parted(whole)
+        linked = onward[2 * local + 1] * coupling[2 * pair + 1].astype(F32)
+        far[local, cross] = wide(linked)
+        far[local, cross_t] = wide(linked.T)
     part = total.reshape(rows // 8, 8, rows).sum(axis=0)
+    exact = functools.partial(jnp.dot, precision=lax.Precision.HIGHEST, preferred_element_type=F32)
 
     @pl.when(step == 0)
     def _():
         trace[...] = part
-        exact = functools.partial(jnp.dot, precision=lax.Precision.HIGHEST, preferred_element_type=F32)
+        near_ends[0] = near[0]
+        far_ends[0] = far[0]
+        beside[0] = near[1, pre[0]]
         first = precond[0]
         edges[2] = first
         edges[3] = exact(exact(first, diag[0]), first)
@@ -111,7 +119,11 @@
 
     @pl.when(step == steps - 1)
     def _():
-        exact = functools.partial(jnp.dot, precision=lax.Precision.HIGHEST, preferred_element_type=F32)
+        near_ends[1] = near[blocks // 2 - 1]
+        far_ends[1] = far[blocks // 2 - 1]
+        beside[1] = near[blocks // 2 - 2, pre[1]]
+        beside[2] = far[blocks // 2 - 2, cross]
+        beside[3] = far[blocks // 2 - 2, cross_t]
         last = onward[blocks - 1] * coupling[steps * blocks - 1].astype(F32)
         mapped = exact(precond[blocks - 1], last)
         edges[0] = exact(last.T, mapped)
@@ -142,10 +154,12 @@
 
 
 def assemble_kernel(
-    targets, received, weights, pair_high, pair_low, cross, cross_t, edges, rhs, theta_out, to_left, to_right, *, eigens
+    targets, received, near_ends, far_ends, beside, edges, near, rhs, theta_out, to_left, to_right, near_held, arrival, *, eigens
 ):
     total = received.shape[0]
     blocks, values, rows = rhs.shape
+    copy = pltpu.make_async_copy(near, near_held, arrival)
+    copy.start()
     rhs[...] = jnp.zeros_like(rhs)
 
     def step(entry, carry):
@@ -158,65 +172,69 @@
     shares = lax.fori_loop(0, total, step, jnp.zeros((EXTRA // 2, rows), F32), unroll=8)
     theta = shares[:1] * (1.0 / eigens)
     theta_out[...] = jnp.broadcast_to(theta, theta_out.shape)
-    pairs = blocks // 2
+
+    weights, high, low, cross, cross_t = layout(rows)
 
     def pre(value, block):
-        return by_wide(tall(value), weights[block])
+        own = beside[block - 2] if block in (2, 3) else near_ends[block // 4, weights[block % 2]]
+        return by_wide(tall(value), own)
 
     both = functools.partial(jnp.concatenate, axis=1)
     first = [rhs[block] for block in range(EDGE)]
     z0 = [pre(first[block], block) for block in range(EDGE)]
-    q1 = by_pair(tall(both(z0[:2])), pair_high[0], pair_low[0]) - both([theta, theta]) * both(first[:2])
-    q1 = [q1[:, :rows], q1[:, rows:] + by_wide(tall(z0[2]), cross_t[0])]
+    q1 = by_pair(tall(both(z0[:2])), near_ends[0, high], far_ends[0, low]) - both([theta, theta]) * both(first[:2])
+    q1 = [q1[:, :rows], q1[:, rows:] + by_wide(tall(z0[2]), far_ends[0, cross_t])]
     z1 = [pre(q1[block], block) for block in range(2)]
-    q2 = by_pair(tall(both(z1)), pair_high[0], pair_low[0])[:, :rows] - theta * q1[0]
+    q2 = by_pair(tall(both(z1)), near_ends[0, high], far_ends[0, low])[:, :rows] - theta * q1[0]
     to_left[0] = z0[0]
     to_left[1] = z1[0]
     to_left[2] = pre(q2, 0)
     last = [rhs[blocks - EDGE + block] for block in range(EDGE)]
-    z0 = [pre(last[block], blocks - EDGE + block) for block in range(EDGE)]
-    q1 = by_pair(tall(both(z0[1:])), pair_high[pairs - 1], pair_low[pairs - 1]) - both([theta, theta]) * both(last[1:])
-    q1 = [q1[:, :rows] + by_wide(tall(z0[0]), cross[pairs - 2]), q1[:, rows:]]
-    z1 = [pre(q1[block], blocks - 2 + block) for block in range(2)]
-    q2 = by_pair(tall(both(z1)), pair_high[pairs - 1], pair_low[pairs - 1])[:, rows:] - theta * q1[1]
-    for place, value in enumerate((z0[2], z1[1], pre(q2, blocks - 1))):
-        to_right[place] = by_wide(tall(value), cross[pairs - 1])
+    z0 = [pre(last[block], EDGE + block) for block in range(EDGE)]
+    q1 = by_pair(tall(both(z0[1:])), near_ends[1, high], far_ends[1, low]) - both([theta, theta]) * both(last[1:])
+    q1 = [q1[:, :rows] + by_wide(tall(z0[0]), beside[2]), q1[:, rows:]]
+    z1 = [pre(q1[block], 4 + block) for block in range(2)]
+    q2 = by_pair(tall(both(z1)), near_ends[1, high], far_ends[1, low])[:, rows:] - theta * q1[1]
+    for place, value in enumerate((z0[2], z1[1], pre(q2, 5))):
+        to_right[place] = by_wide(tall(value), far_ends[1, cross])
     for half in range(2):
         part = slice(half * values, (half + 1) * values)
         to_right[3 + half] = edges[0, part]
         to_right[5 + half] = edges[1, part]
         to_left[3 + half] = edges[2, part]
         to_left[5 + half] = edges[3, part]
-
-
-def basis_kernel(rhs, theta_in, weights, pair_high, pair_low, cross, cross_t, basis, mapped, sums, stacked):
+    copy.wait()
+
+
+def basis_kernel(rhs, theta_in, near, far, basis, mapped, sums, stacked):
     blocks, values, rows = rhs.shape
     pairs = blocks // 2
     theta = theta_in[:1]
     theta_pair = jnp.concatenate([theta, theta], axis=1)
+    weights, high, low, cross, cross_t = layout(rows)
     basis[0] = rhs[...]
 
-    def sweep(level, carry):
+    for level in range(3):
         even = jnp.zeros((values, rows), F32)
         for block in range(blocks):
             value = basis[level, block]
-            image = by_wide(tall(value), weights[block])
+            image = by_wide(tall(value), near[block // 2, weights[block % 2]])
             mapped[level, block] = image
-            high, low = parted(image)
+            image_high, image_low = parted(image)
             side = slice((block % 2) * rows, (block % 2 + 1) * rows)
-            stacked[block // 2, :values, side] = high
-            stacked[block // 2, values:, side] = low
+            stacked[block // 2, :values, side] = image_high
+            stacked[block // 2, values:, side] = image_low
             if EDGE <= block < blocks - EDGE:
                 even = even + value * image
         sums[2 * level] = even
         odd = jnp.zeros((values, rows), F32)
         for pair in range(pairs):
-            image = by_pair(stacked[pair], pair_high[pair], pair_low[pair])
+            image = by_pair(stacked[pair], near[pair, high], far[pair, low])
             sides = [image[:, :rows], image[:, rows:]]
             if pair > 0:
-                sides[0] = sides[0] + by_wide(stacked[pair - 1, :, rows:], cross[pair - 1])
+                sides[0] = sides[0] + by_wide(stacked[pair - 1, :, rows:], far[pair - 1, cross])
             if pair < pairs - 1:
-                sides[1] = sides[1] + by_wide(stacked[pair + 1, :, :rows], cross_t[pair])
+                sides[1] = sides[1] + by_wide(stacked[pair + 1, :, :rows], far[pair, cross_t])
             for side in range(2):
                 block = 2 * pair + side
                 value = sides[side] - theta * basis[level, block]
@@ -224,24 +242,21 @@
                 if EDGE <= block < blocks - EDGE:
                     odd = odd + value * mapped[level, block]
         sums[2 * level + 1] = odd
-        return carry
-
-    lax.fori_loop(0, 3, sweep, 0)
 
 
 def edge_kernel(
-    from_left, from_right, basis, mapped, sums, theta_in, weights, pair_high, pair_low, cross, cross_t,
-    basis_edge, mapped_edge, moments,
+    from_left, from_right, basis, mapped, sums, theta_in, near_ends, far_ends, beside, basis_edge, mapped_edge, moments
 ):
     _, blocks, values, rows = basis.shape
-    pairs = blocks // 2
     theta = theta_in[:1]
 
+    weights, high, low, cross, cross_t = layout(rows)
+
     def pre(value, block):
-        return by_wide(tall(value), weights[block])
+        return by_wide(tall(value), near_ends[block // 4, weights[block % 2]])
 
     def pair_image(first, second, pair):
-        out = by_pair(tall(jnp.concatenate([first, second], axis=1)), pair_high[pair], pair_low[pair])
+        out = by_pair(tall(jnp.concatenate([first, second], axis=1)), near_ends[pair, high], far_ends[pair, low])
         return out[:, :rows], out[:, rows:]
 
     def square(ref, place):
@@ -263,30 +278,29 @@
     dq3 = (
         own - theta * dq2[0] + from_left[2] + by_wide(start, second) + by_wide(tall(z1), mirror),
         after - theta * dq2[1],
-        by_wide(tall(dz2[1]), cross[0]),
+        by_wide(tall(dz2[1]), far_ends[0, cross]),
     )
     changes = [((0, dq1),), ((0, dq2[0]), (1, dq2[1])), ((0, dq3[0]), (1, dq3[1]), (2, dq3[2]))]
     images = [((0, dz1),), ((0, dz2[0]), (1, dz2[1]))]
 
     last = blocks - 1
-    pair = pairs - 1
     mirror = square(from_right, 3)
     second = square(from_right, 5) - theta * mirror
     mirror, second = wide(mirror), wide(second)
-    start = tall(by_wide(tall(mapped[0, last]), cross[pair]))
-    dq1 = by_wide(tall(from_right[0]), cross_t[pair])
-    dz1 = pre(dq1, last)
+    start = tall(by_wide(tall(mapped[0, last]), far_ends[1, cross]))
+    dq1 = by_wide(tall(from_right[0]), far_ends[1, cross_t])
+    dz1 = pre(dq1, 5)
     z1 = mapped[1, last] + dz1
-    before, own = pair_image(none, dz1, pair)
+    before, own = pair_image(none, dz1, 1)
     ahead = from_right[1] + by_wide(start, mirror)
-    dq2 = (own - theta * dq1 + by_wide(tall(ahead), cross_t[pair]), before)
-    dz2 = (pre(dq2[0], last), pre(dq2[1], last - 1))
-    before, own = pair_image(dz2[1], dz2[0], pair)
-    ahead = from_right[2] + by_wide(start, second) + by_wide(tall(by_wide(tall(z1), cross[pair])), mirror)
+    dq2 = (own - theta * dq1 + by_wide(tall(ahead), far_ends[1, cross_t]), before)
+    dz2 = (pre(dq2[0], 5), pre(dq2[1], 4))
+    before, own = pair_image(dz2[1], dz2[0], 1)
+    ahead = from_right[2] + by_wide(start, second) + by_wide(tall(by_wide(tall(z1), far_ends[1, cross])), mirror)
     dq3 = (
-        own - theta * dq2[0] + by_wide(tall(ahead), cross_t[pair]),
+        own - theta * dq2[0] + by_wide(tall(ahead), far_ends[1, cross_t]),
         before - theta * dq2[1],
-        by_wide(tall(dz2[1]), cross_t[pair - 1]),
+        by_wide(tall(dz2[1]), beside[3]),
     )
     changes[0] += ((5, dq1),)
     changes[1] += ((5, dq2[0]), (4, dq2[1]))
@@ -404,6 +418,7 @@
     blocks = mass_diag.shape[0]
     pairs = blocks // 2
     field = (blocks, values, rows)
+    stay = functools.partial(pltpu.with_memory_space_constraint, memory_space=pltpu.HBM)
     unit = 2 * values * rows * rows
 
     outgoing = pl.pallas_call(
@@ -411,65 +426,66 @@
         out_shape=jax.ShapeDtypeStruct((total, values, rows), BF16),
         in_specs=[SCALARS, SCALARS, WHOLE],
         out_specs=WHOLE,
-        compiler_params=params(16),
+        compiler_params=params(10),
         name="pick",
-    )(send_list.reshape(-1), send_count.reshape(-1), history)
+    )(stay(send_list.reshape(-1)), stay(send_count.reshape(-1)), stay(history))
     arrived = lax.all_to_all(outgoing, AXES, split_axis=0, concat_axis=0, tiled=True)
 
     chunk = 8
     matrix = pl.BlockSpec((chunk, rows, rows), lambda step: (step, 0, 0))
-    weights, pair_high, pair_low, cross, cross_t, trace, edges = pl.pallas_call(
+    half = (4 * rows, 2 * rows)
+    near, far, *ends, trace, edges = pl.pallas_call(
         prepare_kernel,
         grid=(blocks // chunk,),
         out_shape=(
-            pltpu.VMEM((blocks, rows, 2 * rows), BF16),
-            pltpu.VMEM((pairs, 2 * rows, 2 * rows), BF16),
-            pltpu.VMEM((pairs, 2 * rows, 2 * rows), BF16),
-            pltpu.VMEM((pairs, rows, 2 * rows), BF16),
-            pltpu.VMEM((pairs, rows, 2 * rows), BF16),
+            pltpu.HBM((pairs,) + half, BF16),
+            pltpu.HBM((pairs,) + half, BF16),
+            pltpu.VMEM((2,) + half, BF16),
+            pltpu.VMEM((2,) + half, BF16),
+            pltpu.VMEM((4, rows, 2 * rows), BF16),
             pltpu.VMEM((8, rows), F32),
             pltpu.VMEM((4, rows, rows), F32),
         ),
         in_specs=[SCALARS, matrix, matrix, matrix],
-        out_specs=(WHOLE,) * 7,
+        out_specs=(pl.BlockSpec((chunk // 2,) + half, lambda step: (step, 0, 0)),) * 2 + (WHOLE,) * 5,
         compiler_params=params(16),
         cost_estimate=cost(0, 28 * 2**20),
         name="prepare",
-    )(coupling, mass_diag, mass_next, precond)
-    operator = (weights, pair_high, pair_low, cross, cross_t)
+    )(coupling, stay(mass_diag), stay(mass_next), stay(precond))
 
     sending = pl.pallas_call(
         mix_kernel,
         out_shape=jax.ShapeDtypeStruct((total, values + EXTRA, rows), jnp.int16),
         in_specs=[SCALARS, WHOLE, WHOLE, WHOLE],
         out_specs=WHOLE,
-        compiler_params=params(16),
+        compiler_params=params(10),
         name="mix",
     )(relay_list.reshape(-1), arrived, mixed_mass, trace)
     received = lax.all_to_all(sending, AXES, split_axis=0, concat_axis=0, tiled=True)
 
-    ends = jax.ShapeDtypeStruct((EDGE + 4, values, rows), F32)
-    rhs, theta, to_left, to_right = pl.pallas_call(
+    packet = jax.ShapeDtypeStruct((EDGE + 4, values, rows), F32)
+    rhs, theta, to_left, to_right, near_held = pl.pallas_call(
         functools.partial(assemble_kernel, eigens=devices * blocks * rows),
-        out_shape=(pltpu.VMEM(field, F32), pltpu.VMEM((8, rows), F32), ends, ends),
-        in_specs=[SCALARS] + [WHOLE] * 7,
-        out_specs=(WHOLE,) * 4,
-        compiler_params=params(16),
+        out_shape=(pltpu.VMEM(field, F32), pltpu.VMEM((8, rows), F32), packet, packet, pltpu.VMEM((pairs,) + half, BF16)),
+        in_specs=[SCALARS] + [WHOLE] * 5 + [AWAY],
+        out_specs=(WHOLE,) * 5,
+        scratch_shapes=[pltpu.SemaphoreType.DMA],
+        compiler_params=params(10),
         name="assemble",
-    )(relay_target.reshape(-1), received, *operator, edges)
+    )(relay_target.reshape(-1), received, *ends, edges, stay(near))
     from_right = shifted(to_left, -1)
     from_left = shifted(to_right, 1)
 
     basis, mapped, sums = pl.pallas_call(
         basis_kernel,
         out_shape=(pltpu.VMEM((4,) + field, F32), pltpu.VMEM((3,) + field, F32), pltpu.VMEM((6, values, rows), F32)),
-        in_specs=[WHOLE] * 7,
+        in_specs=[WHOLE] * 4,
         out_specs=(WHOLE,) * 3,
         scratch_shapes=[pltpu.VMEM((pairs, 2 * values, 2 * rows), BF16)],
-        compiler_params=params(16),
+        compiler_params=params(10),
         cost_estimate=cost(36 * blocks * unit, 32 * 2**20),
         name="basis",
-    )(rhs, theta, *operator)
+    )(rhs, theta, near_held, far)
 
     basis_edge, mapped_edge, moments = pl.pallas_call(
         edge_kernel,
@@ -478,11 +494,11 @@
             pltpu.VMEM((2, 2 * EDGE, values, rows), F32),
             jax.ShapeDtypeStruct((devices, 8, rows), F32),
         ),
-        in_specs=[WHOLE] * 11,
+        in_specs=[WHOLE] * 9,
         out_specs=(WHOLE,) * 3,
-        compiler_params=params(16),
+        compiler_params=params(10),
         name="edge",
-    )(from_left, from_right, basis, mapped, sums, theta, *operator)
+    )(from_left, from_right, basis, mapped, sums, theta, *ends)
     gathered = lax.all_to_all(moments, AXES, split_axis=0, concat_axis=0, tiled=True)
 
     result = pl.BlockSpec((chunk, values, rows), lambda step: (step, 0, 0))
@@ -493,7 +509,7 @@
         in_specs=[WHOLE] * 6,
         out_specs=(result, result),
         scratch_shapes=[pltpu.VMEM((7, values, rows), F32)],
-        compiler_params=params(16),
+        compiler_params=params(10),
         name="combine",
     )(gathered, theta, basis, mapped, basis_edge, mapped_edge)
 

time: 103 us -> 89.1 us (0.87)
  local copies, waits for them, and re-layouts: 24.7 us -> 0.67 us
  Pallas kernels: 27.6 us -> 39.1 us
  blocking collectives: 35.6 us -> 34.4 us
    unnamed x36 -> x10, local copies, waits for them, and re-layouts: 24.7 us -> 0.67 us
    pallas_call x1, Pallas kernels: 4.42 us -> 13.9 us  [body(): pl.pallas_call(prepare_kernel, grid=(blocks // chunk,), out_shape=(pltpu....]
    pallas_call x1, Pallas kernels: 2.51 us -> 4.16 us  [body(): pl.pallas_call(functools.partial(assemble_kernel, eigens=devices * blocks...]
    all_to_all x1, blocking collectives: 22.6 us -> 21.3 us  [body(): lax.all_to_all(sending, AXES, split_axis=0, concat_axis=0, tiled=True)]
  transfers between devices with their start and end apart: 3 -> 3, of which waited for: 1 -> 1; matrix products, arithmetic and copies ran while one was open for 0% -> 0% of each run, Pallas kernels for 15% -> 28%
where the time goes in v1:
time: 89.1 us; the launch traced here: 88.6 us
  Pallas kernels  39.1 us (44%)
  blocking collectives  34.4 us (39%)
  starting transfers between devices  13.5 us (15%)
    all_to_all x1, blocking collectives, body(): lax.all_to_all(sending, AXES, split_axis=0, concat_axis=0, tiled=True)  21.3 us
    pallas_call x1, Pallas kernels, body(): pl.pallas_call(prepare_kernel, grid=(blocks // chunk,), out_shape=(pltpu....  13.9 us
    all_to_all x1, blocking collectives, body(): lax.all_to_all(moments, AXES, split_axis=0, concat_axis=0, tiled=True)  13.1 us
    pallas_call x1, Pallas kernels, body(): pl.pallas_call(basis_kernel, out_shape=(pltpu.VMEM((4,) + field, F32), pl...  11 us
    all_to_all x1, starting transfers between devices, body(): lax.all_to_all(outgoing, AXES, split_axis=0, concat_axis=0, tiled=True)  7.3 us
    ppermute x2, starting transfers between devices, shifted(): lax.ppermute(value, AXES, [(source, source + steps) for source in range(f...  6.2 us
    pallas_call x1, Pallas kernels, body(): pl.pallas_call(combine_kernel, grid=(blocks // chunk,), out_shape=(jax.Sh...  4.44 us
    pallas_call x1, Pallas kernels, body(): pl.pallas_call(functools.partial(assemble_kernel, eigens=devices * blocks...  4.16 us
  transfers between devices with their start and end apart: 3, of which 1 were waited for; matrix products, arithmetic and copies ran while one was open for 0% of the time, Pallas kernels for 28%

profile of v1, /device:TPU:0, one launch (start us, length us, event | category | flops | bytes accessed | tf_op | source)
XLA Modules:
  0.0 88.6 jit_solution(13144000476317779597)
XLA Ops:
  0.6 2.0 %pick.1 = bf16[32,64,128]{2,1,0:T(8,128)(2,1)} custom-call(s32[32]{0:T(128)} %bitcast.6, s32[32]{0:T(128)} %bitcast.7, bf16[32,64,128]{2,1,0:T(8,128)(2,1)} %history.1), custom_call_target="tpu_custom_call" | custom-call | tf_op jit(solution)/shard_map/pick/pallas_call | solution.py:424
  2.6 7.3 %all-to-all-start = ((bf16[32,64,128]{2,1,0:T(8,128)(2,1)}), bf16[32,64,128]{2,1,0:T(8,128)(2,1)S(1)}, u32[]{:S(2)}, u32[]{:S(2)}) async-start(bf16[32,64,128]{2,1,0:T(8,128)(2,1)} %pick.1), calls=%async_computation | async-start | bytes 1048576 | tf_op jit(solution)/shard_map/all_to_all | solution.py:432
  9.9 0.0 copy-start.2
  10.0 0.6 copy-done.2
  10.6 0.0 copy-start.1
  10.6 0.0 copy-start.3
  10.6 0.0 copy-start.4
  10.6 13.9 %prepare.1 = (bf16[32,512,256]{2,1,0:T(8,128)(2,1)}, bf16[32,512,256]{2,1,0:T(8,128)(2,1)}, bf16[2,512,256]{2,1,0:T(8,128)(2,1)S(1)}, bf16[2,512,256]{2,1,0:T(8,...) custom-call(s32[64]{0:T(128)S(1)} %copy-done.2, ...), custom_call_target="tpu_custom_call" | custom-call | bytes 29360128 | tf_op jit(solution)/shard_map/prepare/pallas_call | solution.py:437
  24.5 0.0 all-to-all-done.arrived
  24.5 0.0 copy-done.1
  24.5 0.0 copy-done.3
  24.6 1.7 %mix.1 = s16[32,72,128]{2,1,0:T(8,128)(2,1)S(1)} custom-call(s32[32]{0:T(128)S(1)} %bitcast.4, bf16[32,64,128]{2,1,0:T(8,128)(2,1)S(1)} %all-to-all-done.arrived, bf16[32,128,128]{2,1,0:T(8,128)(2,1)S(1)} %copy-done.1, f32[8,128]{1,0:T(8,128)S(1)} %get-tuple-element.20.trace), custom_call_target="tpu_custom_call" | custom-call | tf_op jit(solution)/shard_map/mix/pallas_call | solution.py:456
  26.3 21.3 %all_to_all.15.received = s16[32,72,128]{2,1,0:T(8,128)(2,1)S(1)} all-to-all(s16[32,72,128]{2,1,0:T(8,128)(2,1)S(1)} %mix.1), channel_id=1, replica_groups=mesh['dom'=8,'sub'=4] {'dom','sub'}, dimensions={0} | all-to-all | bytes 1179648 | tf_op jit(solution)/shard_map/all_to_all | solution.py:464
  47.6 0.0 copy-done.4
  47.6 0.0 copy-start
  47.6 4.2 %assemble.1 = (f32[64,64,128]{2,1,0:T(8,128)S(1)}, f32[8,128]{1,0:T(8,128)S(1)}, f32[7,64,128]{2,1,0:T(8,128)S(1)}, f32[7,64,128]{2,1,0:T(8,128)S(1)}, bf16[32,512,256]{2,1,0:T(8,128)(2,1)S(1)}) custom-call(s32[32]{0:T(128)S(1)} %bitcast.5, s16[32,72,128]{2,1,0:T(8,128)(2,1)S(1)} %all_to_all.15.received, ...), custom_call_target="tpu_custom_call" | custom-call | tf_op jit(solution)/shard_map/assemble/pallas_call | solution.py:467
  51.8 4.7 %collective-permute-start = (f32[7,64,128]{2,1,0:T(8,128)S(1)}, f32[7,64,128]{2,1,0:T(8,128)S(1)}, u32[]{:S(2)}, u32[]{:S(2)}) collective-permute-start(f32[7,64,128]{2,1,0:T(8,128)S(1)} %get-tuple-element.26), channel_id=1, source_target_pairs={{0,1},{1,2},{2,3},{3,4},{4,5},{5,6},{6,7},{7,8},{8,9},{9,10},{10,1... | collective-permute-start | bytes 688136 | tf_op jit(solution)/shard_map/ppermute | solution.py:399
  56.5 1.5 %collective-permute-start.1 = (f32[7,64,128]{2,1,0:T(8,128)S(1)}, f32[7,64,128]{2,1,0:T(8,128)S(1)}, u32[]{:S(2)}, u32[]{:S(2)}) collective-permute-start(f32[7,64,128]{2,1,0:T(8,128)S(1)} %get-tuple-element.27), channel_id=1, source_target_pairs={{1,0},{2,1},{3,2},{4,3},{5,4},{6,5},{7,6},{8,7},{9,8},{10,9},{11,1... | collective-permute-start | bytes 688136 | tf_op jit(solution)/shard_map/ppermute | solution.py:399
  58.0 0.0 copy-done
  58.0 11.0 %basis.1 = (f32[4,64,64,128]{3,2,1,0:T(8,128)S(1)}, f32[3,64,64,128]{3,2,1,0:T(8,128)S(1)}, f32[6,64,128]{2,1,0:T(8,128)S(1)}) custom-call(f32[64,64,128]{2,1,0:T(8,128)S(1)} %get-tuple-element.28.rhs, f32[8,128]{1,0:T(8,128)S(1)} %get-tuple-element.29.theta_in, bf16[32,512,256]{2,1,0:T(8,128)(2,1)S(1)} %get-tuple-element.30.near, ...), custom_call_target="tpu_custom_call" | custom-call | flops 4831838208 | bytes 33554432 | tf_op jit(solution)/shard_map/basis/pallas_call | solution.py:479
  69.0 0.0 collective-permute-done.from_left
  69.0 0.3 collective-permute-done.1.from_right
  69.3 1.8 %edge.1 = (f32[3,6,64,128]{3,2,1,0:T(8,128)S(1)}, f32[2,6,64,128]{3,2,1,0:T(8,128)S(1)}, f32[32,8,128]{2,1,0:T(8,128)S(1)}) custom-call(f32[7,64,128]{2,1,0:T(8,128)S(1)} %collective-permute-done.from_left, f32[7,64,128]{2,1,0:T(8,128)S(1)} %collective-permute-done.1.from_right, f32[4,64,64,128]{3,2,1,0:T(8,128)S(1)} %get-tuple-element.32.basis, ...), custom_call_target="tpu_custom_call" | custom-call | tf_op jit(solution)/shard_map/edge/pallas_call | solution.py:490
  71.1 13.1 %all_to_all.16.moments = f32[32,8,128]{2,1,0:T(8,128)S(1)} all-to-all(f32[32,8,128]{2,1,0:T(8,128)S(1)} %get-tuple-element.35), channel_id=1, replica_groups=mesh['dom'=8,'sub'=4] {'dom','sub'}, dimensions={0} | all-to-all | bytes 262144 | tf_op jit(solution)/shard_map/all_to_all | solution.py:502
  84.2 4.4 %combine.1 = (f32[64,64,128]{2,1,0:T(8,128)}, f32[64,64,128]{2,1,0:T(8,128)}) custom-call(f32[32,8,128]{2,1,0:T(8,128)S(1)} %all_to_all.16.moments, f32[8,128]{1,0:T(8,128)S(1)} %get-tuple-element.29.theta_in, f32[4,64,64,128]{3,2,1,0:T(8,128)S(1)} %get-tuple-element.32.basis, f32[3,64,64,128]{3,2,1,0:T(8,128)S(1)} %get-tuple-element.33.mapped, ...), custom_call_target="tpu_custom_call" | custom-call | tf_op jit(solution)/shard_map/combine/pallas_call | solution.py:505
Async XLA Ops:
  2.6 21.9 %all-to-all-start = ((bf16[32,64,128]{2,1,0:T(8,128)(2,1)}), bf16[32,64,128]{2,1,0:T(8,128)(2,1)S(1)}, u32[]{:S(2)}, u32[]{:S(2)}) async-start(bf16[32,64,128]{2,1,0:T(8,128)(2,1)} %pick.1), calls=%async_computation | async-start | bytes 1048576 | tf_op jit(solution)/shard_map/all_to_all | solution.py:432
  9.9 0.7 copy-start.2
  10.6 13.9 %copy-start.1 = (bf16[32,128,128]{2,1,0:T(8,128)(2,1)S(1)}, bf16[32,128,128]{2,1,0:T(8,128)(2,1)}, u32[]{:S(2)}) copy-start(bf16[32,128,128]{2,1,0:T(8,128)(2,1)} %mixing.1) | copy-start | bytes 3145732
  10.6 13.9 %copy-start.3 = (s32[1,32,1]{1,2,0:T(1,128)S(1)}, s32[1,32,1]{1,2,0:T(1,128)}, u32[]{:S(2)}) copy-start(s32[1,32,1]{1,2,0:T(1,128)} %param.14) | copy-start | bytes 388
  10.6 37.0 %copy-start.4 = (s32[1,32,1]{1,2,0:T(1,128)S(1)}, s32[1,32,1]{1,2,0:T(1,128)}, u32[]{:S(2)}) copy-start(s32[1,32,1]{1,2,0:T(1,128)} %param.15) | copy-start | bytes 388
  47.6 10.4 %copy-start = (bf16[32,512,256]{2,1,0:T(8,128)(2,1)S(1)}, bf16[32,512,256]{2,1,0:T(8,128)(2,1)}, u32[]{:S(2)}) copy-start(bf16[32,512,256]{2,1,0:T(8,128)(2,1)} %get-tuple-element.31.far) | copy-start | bytes 25165828
  51.8 17.3 %collective-permute-start = (f32[7,64,128]{2,1,0:T(8,128)S(1)}, f32[7,64,128]{2,1,0:T(8,128)S(1)}, u32[]{:S(2)}, u32[]{:S(2)}) collective-permute-start(f32[7,64,128]{2,1,0:T(8,128)S(1)} %get-tuple-element.26), channel_id=1, source_target_pairs={{0,1},{1,2},{2,3},{3,4},{4,5},{5,6},{6,7},{7,8},{8,9},{9,10},{10,1... | collective-permute-start | bytes 688136 | tf_op jit(solution)/shard_map/ppermute | solution.py:399
  56.5 12.8 %collective-permute-start.1 = (f32[7,64,128]{2,1,0:T(8,128)S(1)}, f32[7,64,128]{2,1,0:T(8,128)S(1)}, u32[]{:S(2)}, u32[]{:S(2)}) collective-permute-start(f32[7,64,128]{2,1,0:T(8,128)S(1)} %get-tuple-element.27), channel_id=1, source_target_pairs={{1,0},{2,1},{3,2},{4,3},{5,4},{6,5},{7,6},{8,7},{9,8},{10,9},{11,1... | collective-permute-start | bytes 688136 | tf_op jit(solution)/shard_map/ppermute | solution.py:399

commit v2 on v1

v2 whole, which is shorter than its diff:
```python
import functools

import jax
import jax.numpy as jnp
from jax import lax
from jax.experimental import pallas as pl
from jax.experimental.pallas import tpu as pltpu
from jax.sharding import PartitionSpec as P

AXES = ("dom", "sub")
EDGE = 3
EXTRA = 8
OCTAVE = 64.0
FULL = 32766.0
TINY = 1e-37
F32 = jnp.float32
BF16 = jnp.bfloat16
WHOLE = pl.BlockSpec(memory_space=pltpu.VMEM)
AWAY = pl.BlockSpec(memory_space=pl.ANY)
SCALARS = pl.BlockSpec(memory_space=pltpu.SMEM)


def params(mebibytes):
    return pltpu.CompilerParams(vmem_limit_bytes=mebibytes * 2**20)


def cost(flops, moved):
    return pl.CostEstimate(flops=int(flops), bytes_accessed=int(moved), transcendentals=0)


def layout(rows):
    def place(first, count):
        return slice(first * rows, (first + count) * rows)

    return (place(0, 1), place(1, 1)), place(0, 2), place(2, 2), place(0, 1), place(1, 1)


def dot(first, second):
    return jnp.dot(first, second, preferred_element_type=F32)


def parted(value):
    high = value.astype(BF16)
    return high, (value - high.astype(F32)).astype(BF16)


def tall(value):
    return jnp.concatenate(parted(value), axis=0)


def wide(value):
    return jnp.concatenate(parted(value), axis=1)


def by_wide(stacked, weights):
    rows, columns = stacked.shape[0] // 2, weights.shape[1] // 2
    out = dot(stacked, weights)
    return out[:rows, :columns] + (out[rows:, :columns] + out[:rows, columns:])


def by_pair(stacked, high, low):
    rows = stacked.shape[0] // 2
    out = dot(stacked, high)
    return out[:rows] + (out[rows:] + dot(stacked[:rows], low))


def pick_kernel(picks, counts, history, outgoing, *, slots):
    def step(entry, carry):
        live = (entry % slots) < counts[entry // slots]
        block = history[picks[entry]]
        outgoing[entry] = jnp.where(live, block, jnp.zeros_like(block))
        return carry

    total = outgoing.shape[0]
    lax.fori_loop(0, total, step, 0, unroll=8)


def prepare_kernel(coupling, diag, onward, precond, pre, mass, link, pre_ends, mass_ends, link_ends, beside, trace, edges):
    step = pl.program_id(0)
    steps = pl.num_programs(0)
    blocks = diag.shape[0]
    rows = diag.shape[1]
    sides, high, low, plain, turned = layout(rows)
    total = jnp.zeros((rows, rows), F32)
    for local in range(blocks // 2):
        pair = step * (blocks // 2) + local
        for side in range(2):
            own = precond[2 * local + side]
            pre[local, sides[side]] = wide(own)
            total = total + own * diag[2 * local + side]
        linked = onward[2 * local] * coupling[2 * pair].astype(F32)
        whole = jnp.concatenate(
            [
                jnp.concatenate([diag[2 * local], linked], axis=1),
                jnp.concatenate([linked.T, diag[2 * local + 1]], axis=1),
            ],
            axis=0,
        )
        mass[local, high], mass[local, low] = parted(whole)
        linked = onward[2 * local + 1] * coupling[2 * pair + 1].astype(F32)
        link[local, plain] = wide(linked)
        link[local, turned] = wide(linked.T)
    part = total.reshape(rows // 8, 8, rows).sum(axis=0)
    exact = functools.partial(jnp.dot, precision=lax.Precision.HIGHEST, preferred_element_type=F32)

    @pl.when(step == 0)
    def _():
        trace[...] = part
        pre_ends[0] = pre[0]
        mass_ends[0] = mass[0]
        link_ends[0] = link[0]
        beside[0] = pre[1, sides[0]]
        first = precond[0]
        edges[2] = first
        edges[3] = exact(exact(first, diag[0]), first)

    @pl.when(step > 0)
    def _():
        trace[...] += part

    @pl.when(step == steps - 1)
    def _():
        pre_ends[1] = pre[blocks // 2 - 1]
        mass_ends[1] = mass[blocks // 2 - 1]
        link_ends[1] = link[blocks // 2 - 1]
        beside[1] = pre[blocks // 2 - 2, sides[1]]
        beside[2] = link[blocks // 2 - 2, plain]
        beside[3] = link[blocks // 2 - 2, turned]
        last = onward[blocks - 1] * coupling[steps * blocks - 1].astype(F32)
        mapped = exact(precond[blocks - 1], last)
        edges[0] = exact(last.T, mapped)
        edges[1] = exact(mapped.T, exact(diag[blocks - 1], mapped))


def mix_kernel(relay, arrived, mixing, trace, sending):
    total, values, rows = arrived.shape
    entries = trace.shape[0] * trace.shape[1]
    share = jnp.sum(jnp.sum(trace[...], axis=0, keepdims=True), axis=1, keepdims=True)
    share = jnp.maximum(jnp.broadcast_to(share, (1, rows)), TINY)
    share_code = jnp.floor(jnp.log2(share) * OCTAVE).astype(jnp.int32)
    lower = lax.broadcasted_iota(jnp.int32, (EXTRA, rows), 0) < EXTRA // 2

    def step(entry, carry):
        slot = relay[entry]
        tile = dot(arrived[slot], mixing[slot])
        peak = jnp.max(jnp.abs(tile), axis=0, keepdims=True)
        code = jnp.floor(jnp.log2(jnp.maximum(peak, TINY)) * OCTAVE) + 2.0
        scaled = tile * (FULL / jnp.exp2(code * (1.0 / OCTAVE)))
        scaled = jnp.clip(jnp.floor(scaled + 0.5), -32767.0, 32767.0)
        sending[entry, :values] = scaled.astype(jnp.int32).astype(jnp.int16)
        codes = jnp.where(lower, code.astype(jnp.int32), share_code)
        sending[entry, values:] = codes.astype(jnp.int16)
        return carry

    lax.fori_loop(0, total, step, 0, unroll=32)


def assemble_kernel(
    targets, received, pre_ends, mass_ends, link_ends, beside, edges, pre_away, rhs, theta_out, even_packet, odd_packet, pre, arrival, *, eigens
):
    total = received.shape[0]
    blocks, values, rows = rhs.shape
    copy = pltpu.make_async_copy(pre_away, pre, arrival)
    copy.start()
    rhs[...] = jnp.zeros_like(rhs)

    def step(entry, carry):
        extra = jnp.exp2(received[entry, values:].astype(jnp.int32).astype(F32) * (1.0 / OCTAVE))
        tile = received[entry, :values].astype(jnp.int32).astype(F32) * (extra[:1] * (1.0 / FULL))
        block = targets[entry]
        rhs[block] = rhs[block] + tile
        return carry + extra[EXTRA // 2 :]

    shares = lax.fori_loop(0, total, step, jnp.zeros((EXTRA // 2, rows), F32), unroll=8)
    theta = shares[:1] * (1.0 / eigens)
    theta_out[...] = jnp.broadcast_to(theta, theta_out.shape)

    sides, high, low, plain, turned = layout(rows)

    def conditioned(value, block):
        own = beside[block - 2] if block in (2, 3) else pre_ends[block // 4, sides[block % 2]]
        return by_wide(tall(value), own)

    both = functools.partial(jnp.concatenate, axis=1)
    first = [rhs[block] for block in range(EDGE)]
    z0 = [conditioned(first[block], block) for block in range(EDGE)]
    q1 = by_pair(tall(both(z0[:2])), mass_ends[0, high], mass_ends[0, low]) - both([theta, theta]) * both(first[:2])
    q1 = [q1[:, :rows], q1[:, rows:] + by_wide(tall(z0[2]), link_ends[0, turned])]
    z1 = [conditioned(q1[block], block) for block in range(2)]
    q2 = by_pair(tall(both(z1)), mass_ends[0, high], mass_ends[0, low])[:, :rows] - theta * q1[0]
    to_left = [z0[0], z1[0], conditioned(q2, 0)]
    last = [rhs[blocks - EDGE + block] for block in range(EDGE)]
    z0 = [conditioned(last[block], EDGE + block) for block in range(EDGE)]
    q1 = by_pair(tall(both(z0[1:])), mass_ends[1, high], mass_ends[1, low]) - both([theta, theta]) * both(last[1:])
    q1 = [q1[:, :rows] + by_wide(tall(z0[0]), beside[2]), q1[:, rows:]]
    z1 = [conditioned(q1[block], 4 + block) for block in range(2)]
    q2 = by_pair(tall(both(z1)), mass_ends[1, high], mass_ends[1, low])[:, rows:] - theta * q1[1]
    to_right = [by_wide(tall(value), link_ends[1, plain]) for value in (z0[2], z1[1], conditioned(q2, 5))]
    for product in range(4):
        for half in range(2):
            (to_right if product < 2 else to_left).append(edges[product, half * values : (half + 1) * values])
    even = stands_even()
    for entry in range(EDGE + 4):
        even_packet[entry] = jnp.where(even, to_right[entry], to_left[entry])
        odd_packet[entry] = jnp.where(even, to_left[entry], to_right[entry])
    copy.wait()


def basis_kernel(rhs, theta_in, pre, mass, link_away, basis, mapped, sums, stacked, link, arrival):
    blocks, values, rows = rhs.shape
    pairs = blocks // 2
    theta = theta_in[:1]
    theta_pair = jnp.concatenate([theta, theta], axis=1)
    sides, high, low, plain, turned = layout(rows)
    copy = pltpu.make_async_copy(link_away, link, arrival)
    copy.start()
    basis[0] = rhs[...]

    for level in range(3):
        even = jnp.zeros((values, rows), F32)
        for block in range(blocks):
            value = basis[level, block]
            image = by_wide(tall(value), pre[block // 2, sides[block % 2]])
            mapped[level, block] = image
            image_high, image_low = parted(image)
            side = slice((block % 2) * rows, (block % 2 + 1) * rows)
            stacked[block // 2, :values, side] = image_high
            stacked[block // 2, values:, side] = image_low
            if EDGE <= block < blocks - EDGE:
                even = even + value * image
        sums[2 * level] = even
        if level == 0:
            copy.wait()
        odd = jnp.zeros((values, rows), F32)
        for pair in range(pairs):
            image = by_pair(stacked[pair], mass[pair, high], mass[pair, low])
            parts = [image[:, :rows], image[:, rows:]]
            if pair > 0:
                parts[0] = parts[0] + by_wide(stacked[pair - 1, :, rows:], link[pair - 1, plain])
            if pair < pairs - 1:
                parts[1] = parts[1] + by_wide(stacked[pair + 1, :, :rows], link[pair, turned])
            for side in range(2):
                block = 2 * pair + side
                value = parts[side] - theta * basis[level, block]
                basis[level + 1, block] = value
                if EDGE <= block < blocks - EDGE:
                    odd = odd + value * mapped[level, block]
        sums[2 * level + 1] = odd


def edge_kernel(
    even_met, odd_met, basis, mapped, sums, theta_in, pre_ends, mass_ends, link_ends, beside, basis_edge, mapped_edge, moments
):
    _, blocks, values, rows = basis.shape
    theta = theta_in[:1]
    even = stands_even()
    from_left = [jnp.where(even, odd_met[entry], even_met[entry]) for entry in range(EDGE + 4)]
    from_right = [jnp.where(even, even_met[entry], odd_met[entry]) for entry in range(EDGE + 4)]

    sides, high, low, plain, turned = layout(rows)

    def conditioned(value, block):
        return by_wide(tall(value), pre_ends[block // 4, sides[block % 2]])

    def pair_image(first, second, pair):
        out = by_pair(tall(jnp.concatenate([first, second], axis=1)), mass_ends[pair, high], mass_ends[pair, low])
        return out[:, :rows], out[:, rows:]

    def square(ref, place):
        return jnp.concatenate([ref[place], ref[place + 1]], axis=0)

    none = jnp.zeros((values, rows), F32)

    mirror = square(from_left, 3)
    second = square(from_left, 5) - theta * mirror
    mirror, second = wide(mirror), wide(second)
    start = tall(mapped[0, 0])
    dq1 = from_left[0]
    dz1 = conditioned(dq1, 0)
    z1 = mapped[1, 0] + dz1
    own, after = pair_image(dz1, none, 0)
    dq2 = (own - theta * dq1 + from_left[1] + by_wide(start, mirror), after)
    dz2 = (conditioned(dq2[0], 0), conditioned(dq2[1], 1))
    own, after = pair_image(dz2[0], dz2[1], 0)
    dq3 = (
        own - theta * dq2[0] + from_left[2] + by_wide(start, second) + by_wide(tall(z1), mirror),
        after - theta * dq2[1],
        by_wide(tall(dz2[1]), link_ends[0, plain]),
    )
    changes = [((0, dq1),), ((0, dq2[0]), (1, dq2[1])), ((0, dq3[0]), (1, dq3[1]), (2, dq3[2]))]
    images = [((0, dz1),), ((0, dz2[0]), (1, dz2[1]))]

    last = blocks - 1
    mirror = square(from_right, 3)
    second = square(from_right, 5) - theta * mirror
    mirror, second = wide(mirror), wide(second)
    start = tall(by_wide(tall(mapped[0, last]), link_ends[1, plain]))
    dq1 = by_wide(tall(from_right[0]), link_ends[1, turned])
    dz1 = conditioned(dq1, 5)
    z1 = mapped[1, last] + dz1
    before, own = pair_image(none, dz1, 1)
    ahead = from_right[1] + by_wide(start, mirror)
    dq2 = (own - theta * dq1 + by_wide(tall(ahead), link_ends[1, turned]), before)
    dz2 = (conditioned(dq2[0], 5), conditioned(dq2[1], 4))
    before, own = pair_image(dz2[1], dz2[0], 1)
    ahead = from_right[2] + by_wide(start, second) + by_wide(tall(by_wide(tall(z1), link_ends[1, plain])), mirror)
    dq3 = (
        own - theta * dq2[0] + by_wide(tall(ahead), link_ends[1, turned]),
        before - theta * dq2[1],
        by_wide(tall(dz2[1]), beside[3]),
    )
    changes[0] += ((5, dq1),)
    changes[1] += ((5, dq2[0]), (4, dq2[1]))
    changes[2] += ((5, dq3[0]), (4, dq3[1]), (3, dq3[2]))
    images[0] += ((5, dz1),)
    images[1] += ((5, dz2[0]), (4, dz2[1]))

    places = [0, 1, 2, blocks - 3, blocks - 2, blocks - 1]
    before = [rhs_block for rhs_block in (basis[0, block] for block in places)]
    lane = lax.broadcasted_iota(jnp.int32, (values, rows), 1)
    table = none
    for level in range(3):
        image = [mapped[level, block] for block in places]
        if level > 0:
            for spot, change in images[level - 1]:
                image[spot] = image[spot] + change
            for spot in range(2 * EDGE):
                mapped_edge[level - 1, spot] = image[spot]
        now = [basis[level + 1, block] for block in places]
        for spot, change in changes[level]:
            now[spot] = now[spot] + change
        even = sums[2 * level]
        odd = sums[2 * level + 1]
        for spot in range(2 * EDGE):
            basis_edge[level, spot] = now[spot]
            even = even + before[spot] * image[spot]
            odd = odd + now[spot] * image[spot]
        table = jnp.where(lane == 2 * level, jnp.sum(even, axis=1, keepdims=True), table)
        table = jnp.where(lane == 2 * level + 1, jnp.sum(odd, axis=1, keepdims=True), table)
        before = now
    flipped = jnp.concatenate([table, jnp.zeros((rows - values, rows), F32)], axis=0).T[:8]
    for peer in range(moments.shape[0]):
        moments[peer] = flipped


def combine_kernel(moments, theta_in, basis, mapped, basis_edge, mapped_edge, solution, residual, factors):
    step = pl.program_id(0)
    _, blocks, values, rows = basis.shape
    chunk = solution.shape[0]

    @pl.when(step == 0)
    def _():
        total = jnp.sum(moments[...], axis=0)
        theta = theta_in[:1]
        m0, m1, m2, m3, m4, m5 = (total[place : place + 1] for place in range(6))
        m0 = m0 + TINY
        l10 = m1 / m0
        l20 = m2 / m0
        d1 = m2 - l10 * m1 + TINY
        g21 = m3 - l20 * m1
        l21 = g21 / d1
        d2 = m4 - l20 * m2 - l21 * g21 + TINY
        b1 = l10 * m3 - m4
        b2 = l20 * m3 - l21 * b1 - m5
        c2 = b2 / d2
        c1 = b1 / d1 - l21 * c2
        c0 = -m3 / m0 - l10 * c1 - l20 * c2
        scale = 1.0 / (c0 - theta * (c1 - theta * (c2 - theta)))
        c0, c1, c2, c3 = c0 * scale, c1 * scale, c2 * scale, scale
        y2 = -c3
        y1 = -c2 - theta * y2
        y0 = -c1 - theta * y1
        table = jnp.concatenate([c0, c1, c2, c3, y0, y1, y2, jnp.zeros((rows - 7, rows), F32)], axis=0).T
        for place in range(7):
            factors[place] = jnp.broadcast_to(table[:values, place : place + 1], (values, rows))

    def store(first, count, basis_of, mapped_of):
        for row in range(0, values, 8):
            part = slice(row, row + 8)
            factor = [factors[place, part] for place in range(7)]
            for place in range(first, first + count):
                q = basis_of(place, part)
                z = mapped_of(place, part)
                residual[place, part] = (q[0] * factor[0] + q[1] * factor[1]) + (q[2] * factor[2] + q[3] * factor[3])
                solution[place, part] = z[0] * factor[4] + z[1] * factor[5] + z[2] * factor[6]

    store(
        0,
        chunk,
        lambda place, part: [basis[level, step * chunk + place, part] for level in range(4)],
        lambda place, part: [mapped[level, step * chunk + place, part] for level in range(3)],
    )

    def edge(first, block, entry):
        store(
            first,
            EDGE,
            lambda place, part: [basis[0, block - first + place, part]]
            + [basis_edge[level, entry - first + place, part] for level in range(3)],
            lambda place, part: [mapped[0, block - first + place, part]]
            + [mapped_edge[level, entry - first + place, part] for level in range(2)],
        )

    @pl.when(step == 0)
    def _():
        edge(0, 0, 0)

    @pl.when(step == pl.num_programs(0) - 1)
    def _():
        edge(chunk - EDGE, blocks - EDGE, EDGE)


def stands_even():
    return (lax.axis_index(AXES[0]) * lax.axis_size(AXES[1]) + lax.axis_index(AXES[1])) % 2 == 0


def exchanged(value, first):
    swaps = [(one, one + 1) for one in range(first, lax.axis_size(AXES) - 1, 2)]
    return lax.ppermute(value, AXES, swaps + [(other, one) for one, other in swaps])


def body(
    history,
    send_list,
    send_count,
    mixed_mass,
    relay_list,
    relay_target,
    mass_diag,
    mass_next,
    coupling,
    precond,
):
    devices = lax.axis_size(AXES)
    slots = send_list.shape[2]
    total = devices * slots
    values, rows = history.shape[1:]
    blocks = mass_diag.shape[0]
    pairs = blocks // 2
    field = (blocks, values, rows)
    stay = functools.partial(pltpu.with_memory_space_constraint, memory_space=pltpu.HBM)
    unit = 2 * values * rows * rows

    outgoing = pl.pallas_call(
        functools.partial(pick_kernel, slots=slots),
        out_shape=jax.ShapeDtypeStruct((total, values, rows), BF16),
        in_specs=[SCALARS, SCALARS, WHOLE],
        out_specs=WHOLE,
        compiler_params=params(10),
        name="pick",
    )(stay(send_list.reshape(-1)), stay(send_count.reshape(-1)), stay(history))
    arrived = lax.all_to_all(outgoing, AXES, split_axis=0, concat_axis=0, tiled=True)

    chunk = 16
    matrix = pl.BlockSpec((chunk, rows, rows), lambda step: (step, 0, 0))
    pre_part = link_part = (2 * rows, 2 * rows)
    mass_part = (4 * rows, 2 * rows)
    pre, mass, link, *ends, trace, edges = pl.pallas_call(
        prepare_kernel,
        grid=(blocks // chunk,),
        out_shape=(
            *(pltpu.HBM((pairs,) + part, BF16) for part in (pre_part, mass_part, link_part)),
            *(pltpu.VMEM((2,) + part, BF16) for part in (pre_part, mass_part, link_part)),
            pltpu.VMEM((4, rows, 2 * rows), BF16),
            pltpu.VMEM((8, rows), F32),
            pltpu.VMEM((4, rows, rows), F32),
        ),
        in_specs=[SCALARS, matrix, matrix, matrix],
        out_specs=tuple(
            pl.BlockSpec((chunk // 2,) + part, lambda step: (step, 0, 0)) for part in (pre_part, mass_part, link_part)
        )
        + (WHOLE,) * 6,
        compiler_params=params(28),
        cost_estimate=cost(0, 28 * 2**20),
        name="prepare",
    )(stay(coupling), stay(mass_diag), stay(mass_next), stay(precond))

    sending = pl.pallas_call(
        mix_kernel,
        out_shape=jax.ShapeDtypeStruct((total, values + EXTRA, rows), jnp.int16),
        in_specs=[SCALARS, WHOLE, WHOLE, WHOLE],
        out_specs=WHOLE,
        compiler_params=params(10),
        name="mix",
    )(relay_list.reshape(-1), arrived, mixed_mass, trace)
    received = lax.all_to_all(sending, AXES, split_axis=0, concat_axis=0, tiled=True)

    packet = jax.ShapeDtypeStruct((EDGE + 4, values, rows), F32)
    rhs, theta, even_packet, odd_packet, pre_held = pl.pallas_call(
        functools.partial(assemble_kernel, eigens=devices * blocks * rows),
        out_shape=(pltpu.VMEM(field, F32), pltpu.VMEM((8, rows), F32), packet, packet, pltpu.VMEM((pairs,) + pre_part, BF16)),
        in_specs=[SCALARS] + [WHOLE] * 6 + [AWAY],
        out_specs=(WHOLE,) * 5,
        scratch_shapes=[pltpu.SemaphoreType.DMA],
        compiler_params=params(10),
        name="assemble",
    )(relay_target.reshape(-1), received, *ends, edges, stay(pre))
    even_met = exchanged(even_packet, 0)
    odd_met = exchanged(odd_packet, 1)

    basis, mapped, sums = pl.pallas_call(
        basis_kernel,
        out_shape=(pltpu.VMEM((4,) + field, F32), pltpu.VMEM((3,) + field, F32), pltpu.VMEM((6, values, rows), F32)),
        in_specs=[WHOLE] * 4 + [AWAY],
        out_specs=(WHOLE,) * 3,
        scratch_shapes=[
            pltpu.VMEM((pairs, 2 * values, 2 * rows), BF16),
            pltpu.VMEM((pairs,) + link_part, BF16),
            pltpu.SemaphoreType.DMA,
        ],
        compiler_params=params(12),
        cost_estimate=cost(36 * blocks * unit, 32 * 2**20),
        name="basis",
    )(rhs, theta, pre_held, mass, stay(link))

    basis_edge, mapped_edge, moments = pl.pallas_call(
        edge_kernel,
        out_shape=(
            pltpu.VMEM((3, 2 * EDGE, values, rows), F32),
            pltpu.VMEM((2, 2 * EDGE, values, rows), F32),
            jax.ShapeDtypeStruct((devices, 8, rows), F32),
        ),
        in_specs=[WHOLE] * 10,
        out_specs=(WHOLE,) * 3,
        compiler_params=params(10),
        name="edge",
    )(even_met, odd_met, basis, mapped, sums, theta, *ends)
    gathered = lax.all_to_all(moments, AXES, split_axis=0, concat_axis=0, tiled=True)

    chunk = 16
    result = pl.BlockSpec((chunk, values, rows), lambda step: (step, 0, 0))
    return pl.pallas_call(
        combine_kernel,
        grid=(blocks // chunk,),
        out_shape=(jax.ShapeDtypeStruct(field, F32),) * 2,
        in_specs=[WHOLE] * 6,
        out_specs=(result, result),
        scratch_shapes=[pltpu.VMEM((7, values, rows), F32)],
        compiler_params=params(10),
        name="combine",
    )(gathered, theta, basis, mapped, basis_edge, mapped_edge)


def solution(mesh):
    placed = (
        P(AXES, None, None),
        P(AXES, None, None),
        P(AXES, None),
        P(AXES, None, None),
        P(AXES, None, None),
        P(AXES, None, None),
        P(AXES, None, None),
        P(AXES, None, None),
        P(AXES),
        P(AXES, None, None),
    )
    return jax.shard_map(
        body,
        mesh=mesh,
        in_specs=placed,
        out_specs=(P(AXES, None, None), P(AXES, None, None)),
        check_vma=False,
    )
```

time: 89.1 us -> 83.2 us (0.934)
  Pallas kernels: 39.1 us -> 35.3 us
  starting transfers between devices: 13.5 us -> 10.9 us
  waiting for transfers between devices: 0.28 us -> 2.18 us
    ppermute x2, starting transfers between devices: 6.2 us -> 3.59 us  [exchanged(): lax.ppermute(value, AXES, swaps + [(other, one) for one, other in swaps])]
    all_to_all x1, waiting for transfers between devices: 0.01 us -> 2.17 us  [body(): lax.all_to_all(outgoing, AXES, split_axis=0, concat_axis=0, tiled=True)]
    pallas_call x1, Pallas kernels: 13.9 us -> 12.2 us  [body(): pl.pallas_call(prepare_kernel, grid=(blocks // chunk,), out_shape=(*(pltp...]
    all_to_all x1, blocking collectives: 21.3 us -> 19.5 us  [body(): lax.all_to_all(sending, AXES, split_axis=0, concat_axis=0, tiled=True)]
    pallas_call x1, Pallas kernels: 4.16 us -> 2.74 us  [body(): pl.pallas_call(functools.partial(assemble_kernel, eigens=devices * blocks...]
    all_to_all x1, blocking collectives: 13.1 us -> 14.2 us  [body(): lax.all_to_all(moments, AXES, split_axis=0, concat_axis=0, tiled=True)]
  transfers between devices with their start and end apart: 3 -> 3, of which waited for: 1 -> 1; matrix products, arithmetic and copies ran while one was open for 0% -> 0% of each run, Pallas kernels for 28% -> 29%
where the time goes in v2:
time: 83.2 us; the launch traced here: 82.9 us
  Pallas kernels  35.3 us (42%)
  blocking collectives  33.7 us (41%)
  starting transfers between devices  10.9 us (13%)
  waiting for transfers between devices  2.18 us (3%)
    all_to_all x1, blocking collectives, body(): lax.all_to_all(sending, AXES, split_axis=0, concat_axis=0, tiled=True)  19.5 us
    all_to_all x1, blocking collectives, body(): lax.all_to_all(moments, AXES, split_axis=0, concat_axis=0, tiled=True)  14.2 us
    pallas_call x1, Pallas kernels, body(): pl.pallas_call(prepare_kernel, grid=(blocks // chunk,), out_shape=(*(pltp...  12.2 us
    pallas_call x1, Pallas kernels, body(): pl.pallas_call(basis_kernel, out_shape=(pltpu.VMEM((4,) + field, F32), pl...  11.7 us
    all_to_all x1, starting transfers between devices, body(): lax.all_to_all(outgoing, AXES, split_axis=0, concat_axis=0, tiled=True)  7.3 us
    pallas_call x1, Pallas kernels, body(): pl.pallas_call(combine_kernel, grid=(blocks // chunk,), out_shape=(jax.Sh...  3.78 us
    ppermute x2, starting transfers between devices, exchanged(): lax.ppermute(value, AXES, swaps + [(other, one) for one, other in swaps])  3.59 us
    pallas_call x1, Pallas kernels, body(): pl.pallas_call(functools.partial(assemble_kernel, eigens=devices * blocks...  2.74 us
  transfers between devices with their start and end apart: 3, of which 1 were waited for; matrix products, arithmetic and copies ran while one was open for 0% of the time, Pallas kernels for 29%

profile of v2, /device:TPU:0, one launch (start us, length us, event | category | flops | bytes accessed | tf_op | source)
XLA Modules:
  0.0 82.9 jit_solution(4242464876746389152)
XLA Ops:
  0.6 2.0 %pick.1 = bf16[32,64,128]{2,1,0:T(8,128)(2,1)} custom-call(s32[32]{0:T(128)} %bitcast.6, s32[32]{0:T(128)} %bitcast.7, bf16[32,64,128]{2,1,0:T(8,128)(2,1)} %history.1), custom_call_target="tpu_custom_call" | custom-call | tf_op jit(solution)/shard_map/pick/pallas_call | solution.py:444
  2.6 7.3 %all-to-all-start = ((bf16[32,64,128]{2,1,0:T(8,128)(2,1)}), bf16[32,64,128]{2,1,0:T(8,128)(2,1)S(1)}, u32[]{:S(2)}, u32[]{:S(2)}) async-start(bf16[32,64,128]{2,1,0:T(8,128)(2,1)} %pick.1), calls=%async_computation | async-start | bytes 1048576 | tf_op jit(solution)/shard_map/all_to_all | solution.py:452
  9.9 0.0 copy-start.1
  10.0 0.0 copy-start.2
  10.0 0.0 copy-start.3
  10.0 12.2 %prepare.1 = (bf16[32,256,256]{2,1,0:T(8,128)(2,1)}, bf16[32,512,256]{2,1,0:T(8,128)(2,1)}, bf16[32,256,256]{2,1,0:T(8,128)(2,1)}, bf16[2,256,256]{2,1,0:T(8,128...) custom-call(s32[64]{0:T(128)} %coupling.1, ...), custom_call_target="tpu_custom_call" | custom-call | bytes 29360128 | tf_op jit(solution)/shard_map/prepare/pallas_call | solution.py:458
  22.1 2.2 %all-to-all-done.arrived = bf16[32,64,128]{2,1,0:T(8,128)(2,1)S(1)} async-done(((bf16[32,64,128]{2,1,0:T(8,128)(2,1)}), bf16[32,64,128]{2,1,0:T(8,128)(2,1)S(1)}, u32[]{:S(2)}, u32[]{:S(2)}) %all-to-all-start) | async-done | bytes 524320 | tf_op jit(solution)/shard_map/all_to_all | solution.py:452
  24.3 0.0 copy-done.1
  24.3 0.0 copy-done.2
  24.3 0.0 copy-start
  24.3 1.1 %mix.1 = s16[32,72,128]{2,1,0:T(8,128)(2,1)S(1)} custom-call(s32[32]{0:T(128)S(1)} %bitcast.4, bf16[32,64,128]{2,1,0:T(8,128)(2,1)S(1)} %all-to-all-done.arrived, bf16[32,128,128]{2,1,0:T(8,128)(2,1)S(1)} %copy-done.1, f32[8,128]{1,0:T(8,128)S(1)} %get-tuple-element.22.trace), custom_call_target="tpu_custom_call" | custom-call | tf_op jit(solution)/shard_map/mix/pallas_call | solution.py:478
  25.4 19.5 %all_to_all.15.received = s16[32,72,128]{2,1,0:T(8,128)(2,1)S(1)} all-to-all(s16[32,72,128]{2,1,0:T(8,128)(2,1)S(1)} %mix.1), channel_id=1, replica_groups=mesh['dom'=8,'sub'=4] {'dom','sub'}, dimensions={0} | all-to-all | bytes 1179648 | tf_op jit(solution)/shard_map/all_to_all | solution.py:486
  45.0 0.0 copy-done.3
  45.0 2.7 %assemble.1 = (f32[64,64,128]{2,1,0:T(8,128)S(1)}, f32[8,128]{1,0:T(8,128)S(1)}, f32[7,64,128]{2,1,0:T(8,128)S(1)}, f32[7,64,128]{2,1,0:T(8,128)S(1)}, bf16[32,256,256]{2,1,0:T(8,128)(2,1)S(1)}) custom-call(s32[32]{0:T(128)S(1)} %bitcast.5, s16[32,72,128]{2,1,0:T(8,128)(2,1)S(1)} %all_to_all.15.received, ...), custom_call_target="tpu_custom_call" | custom-call | tf_op jit(solution)/shard_map/assemble/pallas_call | solution.py:489
  47.7 2.7 %collective-permute-start = (f32[7,64,128]{2,1,0:T(8,128)S(1)}, f32[7,64,128]{2,1,0:T(8,128)S(1)}, u32[]{:S(2)}, u32[]{:S(2)}) collective-permute-start(f32[7,64,128]{2,1,0:T(8,128)S(1)} %get-tuple-element.29), channel_id=1, source_target_pairs={{0,1},{2,3},{4,5},{6,7},{8,9},{10,11},{12,13},{14,15},{16,17},{18,... | collective-permute-start | bytes 688136 | tf_op jit(solution)/shard_map/ppermute | solution.py:419
  50.5 0.8 %collective-permute-start.1 = (f32[7,64,128]{2,1,0:T(8,128)S(1)}, f32[7,64,128]{2,1,0:T(8,128)S(1)}, u32[]{:S(2)}, u32[]{:S(2)}) collective-permute-start(f32[7,64,128]{2,1,0:T(8,128)S(1)} %get-tuple-element.30), channel_id=1, source_target_pairs={{1,2},{3,4},{5,6},{7,8},{9,10},{11,12},{13,14},{15,16},{17,18},{19... | collective-permute-start | bytes 688136 | tf_op jit(solution)/shard_map/ppermute | solution.py:419
  51.3 0.0 copy-done
  51.3 11.7 %basis.1 = (f32[4,64,64,128]{3,2,1,0:T(8,128)S(1)}, f32[3,64,64,128]{3,2,1,0:T(8,128)S(1)}, f32[6,64,128]{2,1,0:T(8,128)S(1)}) custom-call(f32[64,64,128]{2,1,0:T(8,128)S(1)} %get-tuple-element.31.rhs, f32[8,128]{1,0:T(8,128)S(1)} %get-tuple-element.32.theta_in, bf16[32,256,256]{2,1,0:T(8,128)(2,1)S(1)} %get-tuple-element.33.pre, ...), custom_call_target="tpu_custom_call" | custom-call | flops 4831838208 | bytes 33554432 | tf_op jit(solution)/shard_map/basis/pallas_call | solution.py:501
  63.0 0.0 collective-permute-done.even_met
  63.1 0.0 collective-permute-done.1.odd_met
  63.1 1.8 %edge.1 = (f32[3,6,64,128]{3,2,1,0:T(8,128)S(1)}, f32[2,6,64,128]{3,2,1,0:T(8,128)S(1)}, f32[32,8,128]{2,1,0:T(8,128)S(1)}) custom-call(f32[7,64,128]{2,1,0:T(8,128)S(1)} %collective-permute-done.even_met, f32[7,64,128]{2,1,0:T(8,128)S(1)} %collective-permute-done.1.odd_met, f32[4,64,64,128]{3,2,1,0:T(8,128)S(1)} %get-tuple-element.36.basis, ...), custom_call_target="tpu_custom_call" | custom-call | tf_op jit(solution)/shard_map/edge/pallas_call | solution.py:516
  64.9 14.2 %all_to_all.16.moments = f32[32,8,128]{2,1,0:T(8,128)S(1)} all-to-all(f32[32,8,128]{2,1,0:T(8,128)S(1)} %get-tuple-element.39), channel_id=1, replica_groups=mesh['dom'=8,'sub'=4] {'dom','sub'}, dimensions={0} | all-to-all | bytes 262144 | tf_op jit(solution)/shard_map/all_to_all | solution.py:528
  79.1 3.8 %combine.1 = (f32[64,64,128]{2,1,0:T(8,128)}, f32[64,64,128]{2,1,0:T(8,128)}) custom-call(f32[32,8,128]{2,1,0:T(8,128)S(1)} %all_to_all.16.moments, f32[8,128]{1,0:T(8,128)S(1)} %get-tuple-element.32.theta_in, f32[4,64,64,128]{3,2,1,0:T(8,128)S(1)} %get-tuple-element.36.basis, f32[3,64,64,128]{3,2,1,0:T(8,128)S(1)} %get-tuple-element.37.mapped, ...), custom_call_target="tpu_custom_call" | custom-call | tf_op jit(solution)/shard_map/combine/pallas_call | solution.py:532
Async XLA Ops:
  2.6 21.7 %all-to-all-start = ((bf16[32,64,128]{2,1,0:T(8,128)(2,1)}), bf16[32,64,128]{2,1,0:T(8,128)(2,1)S(1)}, u32[]{:S(2)}, u32[]{:S(2)}) async-start(bf16[32,64,128]{2,1,0:T(8,128)(2,1)} %pick.1), calls=%async_computation | async-start | bytes 1048576 | tf_op jit(solution)/shard_map/all_to_all | solution.py:452
  9.9 14.4 %copy-start.1 = (bf16[32,128,128]{2,1,0:T(8,128)(2,1)S(1)}, bf16[32,128,128]{2,1,0:T(8,128)(2,1)}, u32[]{:S(2)}) copy-start(bf16[32,128,128]{2,1,0:T(8,128)(2,1)} %mixing.1) | copy-start | bytes 3145732
  10.0 14.4 %copy-start.2 = (s32[1,32,1]{1,2,0:T(1,128)S(1)}, s32[1,32,1]{1,2,0:T(1,128)}, u32[]{:S(2)}) copy-start(s32[1,32,1]{1,2,0:T(1,128)} %param.14) | copy-start | bytes 388
  10.0 35.0 %copy-start.3 = (s32[1,32,1]{1,2,0:T(1,128)S(1)}, s32[1,32,1]{1,2,0:T(1,128)}, u32[]{:S(2)}) copy-start(s32[1,32,1]{1,2,0:T(1,128)} %param.15) | copy-start | bytes 388
  24.3 27.0 %copy-start = (bf16[32,512,256]{2,1,0:T(8,128)(2,1)S(1)}, bf16[32,512,256]{2,1,0:T(8,128)(2,1)}, u32[]{:S(2)}) copy-start(bf16[32,512,256]{2,1,0:T(8,128)(2,1)} %get-tuple-element.34.mass) | copy-start | bytes 25165828
  47.7 15.3 %collective-permute-start = (f32[7,64,128]{2,1,0:T(8,128)S(1)}, f32[7,64,128]{2,1,0:T(8,128)S(1)}, u32[]{:S(2)}, u32[]{:S(2)}) collective-permute-start(f32[7,64,128]{2,1,0:T(8,128)S(1)} %get-tuple-element.29), channel_id=1, source_target_pairs={{0,1},{2,3},{4,5},{6,7},{8,9},{10,11},{12,13},{14,15},{16,17},{18,... | collective-permute-start | bytes 688136 | tf_op jit(solution)/shard_map/ppermute | solution.py:419
  50.5 12.6 %collective-permute-start.1 = (f32[7,64,128]{2,1,0:T(8,128)S(1)}, f32[7,64,128]{2,1,0:T(8,128)S(1)}, u32[]{:S(2)}, u32[]{:S(2)}) collective-permute-start(f32[7,64,128]{2,1,0:T(8,128)S(1)} %get-tuple-element.30), channel_id=1, source_target_pairs={{1,2},{3,4},{5,6},{7,8},{9,10},{11,12},{13,14},{15,16},{17,18},{19... | collective-permute-start | bytes 688136 | tf_op jit(solution)/shard_map/ppermute | solution.py:419

commit v3 on v2

--- a/solution.py
+++ b/solution.py
@@ -375,13 +375,14 @@
             factors[place] = jnp.broadcast_to(table[:values, place : place + 1], (values, rows))
 
     def store(first, count, basis_of, mapped_of):
-        for row in range(0, values, 8):
-            part = slice(row, row + 8)
+        for row in range(0, values, 32):
+            part = slice(row, row + 32)
             factor = [factors[place, part] for place in range(7)]
             for place in range(first, first + count):
                 q = basis_of(place, part)
+                residual[place, part] = (q[0] * factor[0] + q[1] * factor[1]) + (q[2] * factor[2] + q[3] * factor[3])
+            for place in range(first, first + count):
                 z = mapped_of(place, part)
-                residual[place, part] = (q[0] * factor[0] + q[1] * factor[1]) + (q[2] * factor[2] + q[3] * factor[3])
                 solution[place, part] = z[0] * factor[4] + z[1] * factor[5] + z[2] * factor[6]
 
     store(

time: 83.2 us -> 82.6 us (level)
  no operation moved by 1% of the time
where the time goes in v3:
time: 82.6 us; the launch traced here: 82.3 us
  Pallas kernels  34.7 us (42%)
  blocking collectives  33.7 us (41%)
  starting transfers between devices  10.9 us (13%)
  waiting for transfers between devices  2.18 us (3%)
    all_to_all x1, blocking collectives, body(): lax.all_to_all(sending, AXES, split_axis=0, concat_axis=0, tiled=True)  19.5 us
    all_to_all x1, blocking collectives, body(): lax.all_to_all(moments, AXES, split_axis=0, concat_axis=0, tiled=True)  14.2 us
    pallas_call x1, Pallas kernels, body(): pl.pallas_call(prepare_kernel, grid=(blocks // chunk,), out_shape=(*(pltp...  12.2 us
    pallas_call x1, Pallas kernels, body(): pl.pallas_call(basis_kernel, out_shape=(pltpu.VMEM((4,) + field, F32), pl...  11.7 us
    all_to_all x1, starting transfers between devices, body(): lax.all_to_all(outgoing, AXES, split_axis=0, concat_axis=0, tiled=True)  7.3 us
    ppermute x2, starting transfers between devices, exchanged(): lax.ppermute(value, AXES, swaps + [(other, one) for one, other in swaps])  3.59 us
    pallas_call x1, Pallas kernels, body(): pl.pallas_call(combine_kernel, grid=(blocks // chunk,), out_shape=(jax.Sh...  3.18 us
    pallas_call x1, Pallas kernels, body(): pl.pallas_call(functools.partial(assemble_kernel, eigens=devices * blocks...  2.74 us
  transfers between devices with their start and end apart: 3, of which 1 were waited for; matrix products, arithmetic and copies ran while one was open for 0% of the time, Pallas kernels for 29%

profile of v3, /device:TPU:0, one launch (start us, length us, event | category | flops | bytes accessed | tf_op | source)
XLA Modules:
  0.0 82.3 jit_solution(603656238088280020)
XLA Ops:
  0.6 2.0 %pick.1 = bf16[32,64,128]{2,1,0:T(8,128)(2,1)} custom-call(s32[32]{0:T(128)} %bitcast.6, s32[32]{0:T(128)} %bitcast.7, bf16[32,64,128]{2,1,0:T(8,128)(2,1)} %history.1), custom_call_target="tpu_custom_call" | custom-call | tf_op jit(solution)/shard_map/pick/pallas_call | solution.py:445
  2.6 7.3 %all-to-all-start = ((bf16[32,64,128]{2,1,0:T(8,128)(2,1)}), bf16[32,64,128]{2,1,0:T(8,128)(2,1)S(1)}, u32[]{:S(2)}, u32[]{:S(2)}) async-start(bf16[32,64,128]{2,1,0:T(8,128)(2,1)} %pick.1), calls=%async_computation | async-start | bytes 1048576 | tf_op jit(solution)/shard_map/all_to_all | solution.py:453
  9.9 0.0 copy-start.1
  10.0 0.0 copy-start.2
  10.0 0.0 copy-start.3
  10.0 12.2 %prepare.1 = (bf16[32,256,256]{2,1,0:T(8,128)(2,1)}, bf16[32,512,256]{2,1,0:T(8,128)(2,1)}, bf16[32,256,256]{2,1,0:T(8,128)(2,1)}, bf16[2,256,256]{2,1,0:T(8,128...) custom-call(s32[64]{0:T(128)} %coupling.1, ...), custom_call_target="tpu_custom_call" | custom-call | bytes 29360128 | tf_op jit(solution)/shard_map/prepare/pallas_call | solution.py:459
  22.1 2.2 %all-to-all-done.arrived = bf16[32,64,128]{2,1,0:T(8,128)(2,1)S(1)} async-done(((bf16[32,64,128]{2,1,0:T(8,128)(2,1)}), bf16[32,64,128]{2,1,0:T(8,128)(2,1)S(1)}, u32[]{:S(2)}, u32[]{:S(2)}) %all-to-all-start) | async-done | bytes 524320 | tf_op jit(solution)/shard_map/all_to_all | solution.py:453
  24.3 0.0 copy-done.1
  24.3 0.0 copy-done.2
  24.3 0.0 copy-start
  24.3 1.1 %mix.1 = s16[32,72,128]{2,1,0:T(8,128)(2,1)S(1)} custom-call(s32[32]{0:T(128)S(1)} %bitcast.4, bf16[32,64,128]{2,1,0:T(8,128)(2,1)S(1)} %all-to-all-done.arrived, bf16[32,128,128]{2,1,0:T(8,128)(2,1)S(1)} %copy-done.1, f32[8,128]{1,0:T(8,128)S(1)} %get-tuple-element.22.trace), custom_call_target="tpu_custom_call" | custom-call | tf_op jit(solution)/shard_map/mix/pallas_call | solution.py:479
  25.4 19.5 %all_to_all.15.received = s16[32,72,128]{2,1,0:T(8,128)(2,1)S(1)} all-to-all(s16[32,72,128]{2,1,0:T(8,128)(2,1)S(1)} %mix.1), channel_id=1, replica_groups=mesh['dom'=8,'sub'=4] {'dom','sub'}, dimensions={0} | all-to-all | bytes 1179648 | tf_op jit(solution)/shard_map/all_to_all | solution.py:487
  45.0 0.0 copy-done.3
  45.0 2.7 %assemble.1 = (f32[64,64,128]{2,1,0:T(8,128)S(1)}, f32[8,128]{1,0:T(8,128)S(1)}, f32[7,64,128]{2,1,0:T(8,128)S(1)}, f32[7,64,128]{2,1,0:T(8,128)S(1)}, bf16[32,256,256]{2,1,0:T(8,128)(2,1)S(1)}) custom-call(s32[32]{0:T(128)S(1)} %bitcast.5, s16[32,72,128]{2,1,0:T(8,128)(2,1)S(1)} %all_to_all.15.received, ...), custom_call_target="tpu_custom_call" | custom-call | tf_op jit(solution)/shard_map/assemble/pallas_call | solution.py:490
  47.7 2.7 %collective-permute-start = (f32[7,64,128]{2,1,0:T(8,128)S(1)}, f32[7,64,128]{2,1,0:T(8,128)S(1)}, u32[]{:S(2)}, u32[]{:S(2)}) collective-permute-start(f32[7,64,128]{2,1,0:T(8,128)S(1)} %get-tuple-element.29), channel_id=1, source_target_pairs={{0,1},{2,3},{4,5},{6,7},{8,9},{10,11},{12,13},{14,15},{16,17},{18,... | collective-permute-start | bytes 688136 | tf_op jit(solution)/shard_map/ppermute | solution.py:420
  50.5 0.8 %collective-permute-start.1 = (f32[7,64,128]{2,1,0:T(8,128)S(1)}, f32[7,64,128]{2,1,0:T(8,128)S(1)}, u32[]{:S(2)}, u32[]{:S(2)}) collective-permute-start(f32[7,64,128]{2,1,0:T(8,128)S(1)} %get-tuple-element.30), channel_id=1, source_target_pairs={{1,2},{3,4},{5,6},{7,8},{9,10},{11,12},{13,14},{15,16},{17,18},{19... | collective-permute-start | bytes 688136 | tf_op jit(solution)/shard_map/ppermute | solution.py:420
  51.3 0.0 copy-done
  51.3 11.7 %basis.1 = (f32[4,64,64,128]{3,2,1,0:T(8,128)S(1)}, f32[3,64,64,128]{3,2,1,0:T(8,128)S(1)}, f32[6,64,128]{2,1,0:T(8,128)S(1)}) custom-call(f32[64,64,128]{2,1,0:T(8,128)S(1)} %get-tuple-element.31.rhs, f32[8,128]{1,0:T(8,128)S(1)} %get-tuple-element.32.theta_in, bf16[32,256,256]{2,1,0:T(8,128)(2,1)S(1)} %get-tuple-element.33.pre, ...), custom_call_target="tpu_custom_call" | custom-call | flops 4831838208 | bytes 33554432 | tf_op jit(solution)/shard_map/basis/pallas_call | solution.py:502
  63.0 0.0 collective-permute-done.even_met
  63.1 0.0 collective-permute-done.1.odd_met
  63.1 1.8 %edge.1 = (f32[3,6,64,128]{3,2,1,0:T(8,128)S(1)}, f32[2,6,64,128]{3,2,1,0:T(8,128)S(1)}, f32[32,8,128]{2,1,0:T(8,128)S(1)}) custom-call(f32[7,64,128]{2,1,0:T(8,128)S(1)} %collective-permute-done.even_met, f32[7,64,128]{2,1,0:T(8,128)S(1)} %collective-permute-done.1.odd_met, f32[4,64,64,128]{3,2,1,0:T(8,128)S(1)} %get-tuple-element.36.basis, ...), custom_call_target="tpu_custom_call" | custom-call | tf_op jit(solution)/shard_map/edge/pallas_call | solution.py:517
  64.9 14.2 %all_to_all.16.moments = f32[32,8,128]{2,1,0:T(8,128)S(1)} all-to-all(f32[32,8,128]{2,1,0:T(8,128)S(1)} %get-tuple-element.39), channel_id=1, replica_groups=mesh['dom'=8,'sub'=4] {'dom','sub'}, dimensions={0} | all-to-all | bytes 262144 | tf_op jit(solution)/shard_map/all_to_all | solution.py:529
  79.1 3.2 %combine.1 = (f32[64,64,128]{2,1,0:T(8,128)}, f32[64,64,128]{2,1,0:T(8,128)}) custom-call(f32[32,8,128]{2,1,0:T(8,128)S(1)} %all_to_all.16.moments, f32[8,128]{1,0:T(8,128)S(1)} %get-tuple-element.32.theta_in, f32[4,64,64,128]{3,2,1,0:T(8,128)S(1)} %get-tuple-element.36.basis, f32[3,64,64,128]{3,2,1,0:T(8,128)S(1)} %get-tuple-element.37.mapped, ...), custom_call_target="tpu_custom_call" | custom-call | tf_op jit(solution)/shard_map/combine/pallas_call | solution.py:533
Async XLA Ops:
  2.6 21.7 %all-to-all-start = ((bf16[32,64,128]{2,1,0:T(8,128)(2,1)}), bf16[32,64,128]{2,1,0:T(8,128)(2,1)S(1)}, u32[]{:S(2)}, u32[]{:S(2)}) async-start(bf16[32,64,128]{2,1,0:T(8,128)(2,1)} %pick.1), calls=%async_computation | async-start | bytes 1048576 | tf_op jit(solution)/shard_map/all_to_all | solution.py:453
  9.9 14.4 %copy-start.1 = (bf16[32,128,128]{2,1,0:T(8,128)(2,1)S(1)}, bf16[32,128,128]{2,1,0:T(8,128)(2,1)}, u32[]{:S(2)}) copy-start(bf16[32,128,128]{2,1,0:T(8,128)(2,1)} %mixing.1) | copy-start | bytes 3145732
  10.0 14.4 %copy-start.2 = (s32[1,32,1]{1,2,0:T(1,128)S(1)}, s32[1,32,1]{1,2,0:T(1,128)}, u32[]{:S(2)}) copy-start(s32[1,32,1]{1,2,0:T(1,128)} %param.14) | copy-start | bytes 388
  10.0 35.0 %copy-start.3 = (s32[1,32,1]{1,2,0:T(1,128)S(1)}, s32[1,32,1]{1,2,0:T(1,128)}, u32[]{:S(2)}) copy-start(s32[1,32,1]{1,2,0:T(1,128)} %param.15) | copy-start | bytes 388
  24.3 27.0 %copy-start = (bf16[32,512,256]{2,1,0:T(8,128)(2,1)S(1)}, bf16[32,512,256]{2,1,0:T(8,128)(2,1)}, u32[]{:S(2)}) copy-start(bf16[32,512,256]{2,1,0:T(8,128)(2,1)} %get-tuple-element.34.mass) | copy-start | bytes 25165828
  47.7 15.3 %collective-permute-start = (f32[7,64,128]{2,1,0:T(8,128)S(1)}, f32[7,64,128]{2,1,0:T(8,128)S(1)}, u32[]{:S(2)}, u32[]{:S(2)}) collective-permute-start(f32[7,64,128]{2,1,0:T(8,128)S(1)} %get-tuple-element.29), channel_id=1, source_target_pairs={{0,1},{2,3},{4,5},{6,7},{8,9},{10,11},{12,13},{14,15},{16,17},{18,... | collective-permute-start | bytes 688136 | tf_op jit(solution)/shard_map/ppermute | solution.py:420
  50.5 12.6 %collective-permute-start.1 = (f32[7,64,128]{2,1,0:T(8,128)S(1)}, f32[7,64,128]{2,1,0:T(8,128)S(1)}, u32[]{:S(2)}, u32[]{:S(2)}) collective-permute-start(f32[7,64,128]{2,1,0:T(8,128)S(1)} %get-tuple-element.30), channel_id=1, source_target_pairs={{1,2},{3,4},{5,6},{7,8},{9,10},{11,12},{13,14},{15,16},{17,18},{19... | collective-permute-start | bytes 688136 | tf_op jit(solution)/shard_map/ppermute | solution.py:420

commit v4 on v3

--- a/solution.py
+++ b/solution.py
@@ -375,8 +375,8 @@
             factors[place] = jnp.broadcast_to(table[:values, place : place + 1], (values, rows))
 
     def store(first, count, basis_of, mapped_of):
-        for row in range(0, values, 32):
-            part = slice(row, row + 32)
+        for row in range(0, values, 64):
+            part = slice(row, row + 64)
             factor = [factors[place, part] for place in range(7)]
             for place in range(first, first + count):
                 q = basis_of(place, part)

time: 82.6 us -> 82.6 us (level)
  no operation moved by 1% of the time
where the time goes in v4:
time: 82.6 us; the launch traced here: 82.3 us
  Pallas kernels  34.7 us (42%)
  blocking collectives  33.7 us (41%)
  starting transfers between devices  10.9 us (13%)
  waiting for transfers between devices  2.18 us (3%)
    all_to_all x1, blocking collectives, body(): lax.all_to_all(sending, AXES, split_axis=0, concat_axis=0, tiled=True)  19.5 us
    all_to_all x1, blocking collectives, body(): lax.all_to_all(moments, AXES, split_axis=0, concat_axis=0, tiled=True)  14.2 us
    pallas_call x1, Pallas kernels, body(): pl.pallas_call(prepare_kernel, grid=(blocks // chunk,), out_shape=(*(pltp...  12.2 us
    pallas_call x1, Pallas kernels, body(): pl.pallas_call(basis_kernel, out_shape=(pltpu.VMEM((4,) + field, F32), pl...  11.7 us
    all_to_all x1, starting transfers between devices, body(): lax.all_to_all(outgoing, AXES, split_axis=0, concat_axis=0, tiled=True)  7.3 us
    ppermute x2, starting transfers between devices, exchanged(): lax.ppermute(value, AXES, swaps + [(other, one) for one, other in swaps])  3.59 us
    pallas_call x1, Pallas kernels, body(): pl.pallas_call(combine_kernel, grid=(blocks // chunk,), out_shape=(jax.Sh...  3.18 us
    pallas_call x1, Pallas kernels, body(): pl.pallas_call(functools.partial(assemble_kernel, eigens=devices * blocks...  2.74 us
  transfers between devices with their start and end apart: 3, of which 1 were waited for; matrix products, arithmetic and copies ran while one was open for 0% of the time, Pallas kernels for 29%

profile of v4, /device:TPU:0, one launch (start us, length us, event | category | flops | bytes accessed | tf_op | source)
XLA Modules:
  0.0 82.3 jit_solution(1011813850775050013)
XLA Ops:
  0.6 2.0 %pick.1 = bf16[32,64,128]{2,1,0:T(8,128)(2,1)} custom-call(s32[32]{0:T(128)} %bitcast.6, s32[32]{0:T(128)} %bitcast.7, bf16[32,64,128]{2,1,0:T(8,128)(2,1)} %history.1), custom_call_target="tpu_custom_call" | custom-call | tf_op jit(solution)/shard_map/pick/pallas_call | solution.py:445
  2.6 7.3 %all-to-all-start = ((bf16[32,64,128]{2,1,0:T(8,128)(2,1)}), bf16[32,64,128]{2,1,0:T(8,128)(2,1)S(1)}, u32[]{:S(2)}, u32[]{:S(2)}) async-start(bf16[32,64,128]{2,1,0:T(8,128)(2,1)} %pick.1), calls=%async_computation | async-start | bytes 1048576 | tf_op jit(solution)/shard_map/all_to_all | solution.py:453
  9.9 0.0 copy-start.1
  10.0 0.0 copy-start.2
  10.0 0.0 copy-start.3
  10.0 12.2 %prepare.1 = (bf16[32,256,256]{2,1,0:T(8,128)(2,1)}, bf16[32,512,256]{2,1,0:T(8,128)(2,1)}, bf16[32,256,256]{2,1,0:T(8,128)(2,1)}, bf16[2,256,256]{2,1,0:T(8,128...) custom-call(s32[64]{0:T(128)} %coupling.1, ...), custom_call_target="tpu_custom_call" | custom-call | bytes 29360128 | tf_op jit(solution)/shard_map/prepare/pallas_call | solution.py:459
  22.1 2.2 %all-to-all-done.arrived = bf16[32,64,128]{2,1,0:T(8,128)(2,1)S(1)} async-done(((bf16[32,64,128]{2,1,0:T(8,128)(2,1)}), bf16[32,64,128]{2,1,0:T(8,128)(2,1)S(1)}, u32[]{:S(2)}, u32[]{:S(2)}) %all-to-all-start) | async-done | bytes 524320 | tf_op jit(solution)/shard_map/all_to_all | solution.py:453
  24.3 0.0 copy-done.1
  24.3 0.0 copy-done.2
  24.3 0.0 copy-start
  24.3 1.1 %mix.1 = s16[32,72,128]{2,1,0:T(8,128)(2,1)S(1)} custom-call(s32[32]{0:T(128)S(1)} %bitcast.4, bf16[32,64,128]{2,1,0:T(8,128)(2,1)S(1)} %all-to-all-done.arrived, bf16[32,128,128]{2,1,0:T(8,128)(2,1)S(1)} %copy-done.1, f32[8,128]{1,0:T(8,128)S(1)} %get-tuple-element.22.trace), custom_call_target="tpu_custom_call" | custom-call | tf_op jit(solution)/shard_map/mix/pallas_call | solution.py:479
  25.4 19.5 %all_to_all.15.received = s16[32,72,128]{2,1,0:T(8,128)(2,1)S(1)} all-to-all(s16[32,72,128]{2,1,0:T(8,128)(2,1)S(1)} %mix.1), channel_id=1, replica_groups=mesh['dom'=8,'sub'=4] {'dom','sub'}, dimensions={0} | all-to-all | bytes 1179648 | tf_op jit(solution)/shard_map/all_to_all | solution.py:487
  45.0 0.0 copy-done.3
  45.0 2.7 %assemble.1 = (f32[64,64,128]{2,1,0:T(8,128)S(1)}, f32[8,128]{1,0:T(8,128)S(1)}, f32[7,64,128]{2,1,0:T(8,128)S(1)}, f32[7,64,128]{2,1,0:T(8,128)S(1)}, bf16[32,256,256]{2,1,0:T(8,128)(2,1)S(1)}) custom-call(s32[32]{0:T(128)S(1)} %bitcast.5, s16[32,72,128]{2,1,0:T(8,128)(2,1)S(1)} %all_to_all.15.received, ...), custom_call_target="tpu_custom_call" | custom-call | tf_op jit(solution)/shard_map/assemble/pallas_call | solution.py:490
  47.7 2.7 %collective-permute-start = (f32[7,64,128]{2,1,0:T(8,128)S(1)}, f32[7,64,128]{2,1,0:T(8,128)S(1)}, u32[]{:S(2)}, u32[]{:S(2)}) collective-permute-start(f32[7,64,128]{2,1,0:T(8,128)S(1)} %get-tuple-element.29), channel_id=1, source_target_pairs={{0,1},{2,3},{4,5},{6,7},{8,9},{10,11},{12,13},{14,15},{16,17},{18,... | collective-permute-start | bytes 688136 | tf_op jit(solution)/shard_map/ppermute | solution.py:420
  50.5 0.8 %collective-permute-start.1 = (f32[7,64,128]{2,1,0:T(8,128)S(1)}, f32[7,64,128]{2,1,0:T(8,128)S(1)}, u32[]{:S(2)}, u32[]{:S(2)}) collective-permute-start(f32[7,64,128]{2,1,0:T(8,128)S(1)} %get-tuple-element.30), channel_id=1, source_target_pairs={{1,2},{3,4},{5,6},{7,8},{9,10},{11,12},{13,14},{15,16},{17,18},{19... | collective-permute-start | bytes 688136 | tf_op jit(solution)/shard_map/ppermute | solution.py:420
  51.3 0.0 copy-done
  51.3 11.7 %basis.1 = (f32[4,64,64,128]{3,2,1,0:T(8,128)S(1)}, f32[3,64,64,128]{3,2,1,0:T(8,128)S(1)}, f32[6,64,128]{2,1,0:T(8,128)S(1)}) custom-call(f32[64,64,128]{2,1,0:T(8,128)S(1)} %get-tuple-element.31.rhs, f32[8,128]{1,0:T(8,128)S(1)} %get-tuple-element.32.theta_in, bf16[32,256,256]{2,1,0:T(8,128)(2,1)S(1)} %get-tuple-element.33.pre, ...), custom_call_target="tpu_custom_call" | custom-call | flops 4831838208 | bytes 33554432 | tf_op jit(solution)/shard_map/basis/pallas_call | solution.py:502
  63.0 0.0 collective-permute-done.even_met
  63.1 0.0 collective-permute-done.1.odd_met
  63.1 1.8 %edge.1 = (f32[3,6,64,128]{3,2,1,0:T(8,128)S(1)}, f32[2,6,64,128]{3,2,1,0:T(8,128)S(1)}, f32[32,8,128]{2,1,0:T(8,128)S(1)}) custom-call(f32[7,64,128]{2,1,0:T(8,128)S(1)} %collective-permute-done.even_met, f32[7,64,128]{2,1,0:T(8,128)S(1)} %collective-permute-done.1.odd_met, f32[4,64,64,128]{3,2,1,0:T(8,128)S(1)} %get-tuple-element.36.basis, ...), custom_call_target="tpu_custom_call" | custom-call | tf_op jit(solution)/shard_map/edge/pallas_call | solution.py:517
  64.9 14.2 %all_to_all.16.moments = f32[32,8,128]{2,1,0:T(8,128)S(1)} all-to-all(f32[32,8,128]{2,1,0:T(8,128)S(1)} %get-tuple-element.39), channel_id=1, replica_groups=mesh['dom'=8,'sub'=4] {'dom','sub'}, dimensions={0} | all-to-all | bytes 262144 | tf_op jit(solution)/shard_map/all_to_all | solution.py:529
  79.1 3.2 %combine.1 = (f32[64,64,128]{2,1,0:T(8,128)}, f32[64,64,128]{2,1,0:T(8,128)}) custom-call(f32[32,8,128]{2,1,0:T(8,128)S(1)} %all_to_all.16.moments, f32[8,128]{1,0:T(8,128)S(1)} %get-tuple-element.32.theta_in, f32[4,64,64,128]{3,2,1,0:T(8,128)S(1)} %get-tuple-element.36.basis, f32[3,64,64,128]{3,2,1,0:T(8,128)S(1)} %get-tuple-element.37.mapped, ...), custom_call_target="tpu_custom_call" | custom-call | tf_op jit(solution)/shard_map/combine/pallas_call | solution.py:533
Async XLA Ops:
  2.6 21.7 %all-to-all-start = ((bf16[32,64,128]{2,1,0:T(8,128)(2,1)}), bf16[32,64,128]{2,1,0:T(8,128)(2,1)S(1)}, u32[]{:S(2)}, u32[]{:S(2)}) async-start(bf16[32,64,128]{2,1,0:T(8,128)(2,1)} %pick.1), calls=%async_computation | async-start | bytes 1048576 | tf_op jit(solution)/shard_map/all_to_all | solution.py:453
  9.9 14.4 %copy-start.1 = (bf16[32,128,128]{2,1,0:T(8,128)(2,1)S(1)}, bf16[32,128,128]{2,1,0:T(8,128)(2,1)}, u32[]{:S(2)}) copy-start(bf16[32,128,128]{2,1,0:T(8,128)(2,1)} %mixing.1) | copy-start | bytes 3145732
  10.0 14.4 %copy-start.2 = (s32[1,32,1]{1,2,0:T(1,128)S(1)}, s32[1,32,1]{1,2,0:T(1,128)}, u32[]{:S(2)}) copy-start(s32[1,32,1]{1,2,0:T(1,128)} %param.14) | copy-start | bytes 388
  10.0 35.0 %copy-start.3 = (s32[1,32,1]{1,2,0:T(1,128)S(1)}, s32[1,32,1]{1,2,0:T(1,128)}, u32[]{:S(2)}) copy-start(s32[1,32,1]{1,2,0:T(1,128)} %param.15) | copy-start | bytes 388
  24.3 27.0 %copy-start = (bf16[32,512,256]{2,1,0:T(8,128)(2,1)S(1)}, bf16[32,512,256]{2,1,0:T(8,128)(2,1)}, u32[]{:S(2)}) copy-start(bf16[32,512,256]{2,1,0:T(8,128)(2,1)} %get-tuple-element.34.mass) | copy-start | bytes 25165828
  47.7 15.3 %collective-permute-start = (f32[7,64,128]{2,1,0:T(8,128)S(1)}, f32[7,64,128]{2,1,0:T(8,128)S(1)}, u32[]{:S(2)}, u32[]{:S(2)}) collective-permute-start(f32[7,64,128]{2,1,0:T(8,128)S(1)} %get-tuple-element.29), channel_id=1, source_target_pairs={{0,1},{2,3},{4,5},{6,7},{8,9},{10,11},{12,13},{14,15},{16,17},{18,... | collective-permute-start | bytes 688136 | tf_op jit(solution)/shard_map/ppermute | solution.py:420
  50.5 12.6 %collective-permute-start.1 = (f32[7,64,128]{2,1,0:T(8,128)S(1)}, f32[7,64,128]{2,1,0:T(8,128)S(1)}, u32[]{:S(2)}, u32[]{:S(2)}) collective-permute-start(f32[7,64,128]{2,1,0:T(8,128)S(1)} %get-tuple-element.30), channel_id=1, source_target_pairs={{1,2},{3,4},{5,6},{7,8},{9,10},{11,12},{13,14},{15,16},{17,18},{19... | collective-permute-start | bytes 688136 | tf_op jit(solution)/shard_map/ppermute | solution.py:420
